TPU v7x, 32 devices: a whole 2x2x4 slice. The times are simulated.
32 devices in a mesh: wave: 8 (over y, x, core), lev: 4 (over z).
Axes of the slice: x: 2, y: 2, z: 4, core: 2. Of those that a mesh axis runs over, the one named last changes fastest.
Arguments:
- grid_fields: float32 [8, 3, 4096, 512], P(None, None, ('wave', 'lev')), may hold values from -6 to 6
- diffusivity: bfloat16 [7, 4096, 512], P(None, ('wave', 'lev')), may hold values from 0.049804688 to 20
- tile_map: int32 [4096], replicated, may hold values from -1 to 7039, as said below
- pair_order: int32 [640], replicated, may hold values from 0 to 639, as said below
- m_order: int32 [320], replicated, may hold values from 0 to 319, each once
- legendre: bfloat16 [320, 641, 640], P('wave'), may hold values from -0.25 to 0.25
Outputs:
- spectral: float32 [320, 2, 3, 8, 641], P('wave', None, None, 'lev')
- fourier_out: bfloat16 [640, 2, 2, 3, 8, 640], P('wave', None, None, None, 'lev')
Inputs may be any that keep to these rules, and one draw needn't show every extreme that they name: `tile_map`: slot s of device d (the linear index over wave and lev, wave first) is entry d * 128 + s; it holds a tile of a pair owned by wave device s // 16, or -1. Each tile p * 11 + b with b * 256 < 4 p + 20 stands in exactly one slot; no other tile appears. A permutation. Wave device w owns pair_order[w * 80 + j] for j < 80, and that pair lies in j * 8 to (j + 1) * 8 - 1. Wave device w owns the wavenumber pairs m_order[w * 40 + j], each q standing for waves q and 639 - q.
All inputs are finite; a program needn't handle non-finite values.
Results may differ from a plain program's by a relative error of at most 0.0073.
Values may be sent and summed in bfloat16 or wider, within the bound.
No kernel may reach another device: no remote copies, remote signals or barrier semaphores. Data moves between devices by JAX's collectives and lax.ppermute only.
A program may use at most 384 MiB of HBM per device.

v0:
```python
import functools

import jax
import jax.numpy as jnp
from jax import lax
from jax.experimental import pallas as pl
from jax.experimental.pallas import tpu as pltpu
from jax.sharding import PartitionSpec as P

TILE = 256
BLK = 11
LANE = 128
ROWS = 16
GROUP = 8
F32 = jnp.float32
BF16 = jnp.bfloat16
MIB = 1024 * 1024
CHUNKS = ((0, 1, 2, 3, 4),)


def params(mib):
    return pltpu.CompilerParams(vmem_limit_bytes=mib * MIB)


def cost(flops, moved):
    return pl.CostEstimate(flops=int(flops), bytes_accessed=int(moved), transcendentals=0)


def row_order(lf):
    full = 2 * lf
    head = full // 8 * 8
    rows = []
    for start in range(0, head, 8):
        for kind in range(2):
            rows += [(kind, start + i) for i in range(8)]
    rest = full - head
    assert 2 * rest == 8 and head == 8
    for kind in range(2):
        rows += [(kind, head + i) for i in range(rest)]
    return rows


def swap_blocks(items, width):
    items = list(items)
    lane = lax.broadcasted_iota(jnp.int32, items[0].shape, 1)
    step = 1
    while step < len(items):
        reach = width * step
        low = (lane & reach) == 0
        for i in range(len(items)):
            if i & step:
                continue
            first, second = items[i], items[i + step]
            items[i] = jnp.where(low, first, pltpu.roll(second, reach, 1))
            items[i + step] = jnp.where(low, pltpu.roll(first, LANE - reach, 1), second)
        step *= 2
    return items


def diffuse_kernel(share, x_ref, a_ref, o_ref):
    levels, fields = x_ref.shape[0], x_ref.shape[1]
    width = x_ref.shape[-1]
    for start in range(0, width, LANE):
        cut = pl.ds(start, LANE)
        coef = [a_ref[k, 0, :, cut].astype(F32) for k in range(levels - 1)]
        ratios = []
        partials = [[] for _ in range(fields)]
        for k in range(levels):
            if k == 0:
                pivot = 1.0 + coef[0]
            elif k == levels - 1:
                pivot = 1.0 + coef[k - 1] - coef[k - 1] * ratios[k - 1]
            else:
                pivot = 1.0 + coef[k - 1] + coef[k] - coef[k - 1] * ratios[k - 1]
            inverse = 1.0 / pivot
            if k < levels - 1:
                ratios.append(coef[k] * inverse)
            for f in range(fields):
                value = x_ref[k, f, 0, :, cut]
                if k:
                    value = value + coef[k - 1] * partials[f][k - 1]
                partials[f].append(value * inverse)
        for f in range(fields):
            solved = None
            for k in range(levels - 1, -1, -1):
                solved = partials[f][k] if solved is None else partials[f][k] + ratios[k] * solved
                o_ref[0, k // share, k % share, f, :, cut] = solved.astype(BF16)


def diffuse(grid_fields, diffusivity, waves, groups):
    levels, fields, slots, width = grid_fields.shape
    cap = slots // waves
    share = levels // groups
    x = grid_fields.reshape(levels, fields, waves, cap, width)
    a = diffusivity.reshape(levels - 1, waves, cap, width)
    return pl.pallas_call(
        functools.partial(diffuse_kernel, share),
        grid=(waves,),
        in_specs=[
            pl.BlockSpec((levels, fields, 1, cap, width), lambda w: (0, 0, w, 0, 0)),
            pl.BlockSpec((levels - 1, 1, cap, width), lambda w: (0, w, 0, 0)),
        ],
        out_specs=pl.BlockSpec((1, groups, share, fields, cap, width), lambda w: (w, 0, 0, 0, 0, 0)),
        out_shape=jax.ShapeDtypeStruct((waves, groups, share, fields, cap, width), BF16),
        compiler_params=params(32),
        cost_estimate=cost(40 * x.size, 6 * x.size + 2 * a.size),
        name="diffuse",
    )(x, a)


def turn(x, count, inverse):
    rest = x - count * jnp.floor(x * inverse)
    quarters = rest * (4.0 * inverse)
    near = jnp.floor(quarters + 0.5)
    angle = (quarters - near) * 1.5707963267948966
    square = angle * angle
    sine = angle * (
        1.0 + square * (-1.0 / 6 + square * (1.0 / 120 + square * (-1.0 / 5040 + square / 362880)))
    )
    cosine = 1.0 + square * (
        -0.5 + square * (1.0 / 24 + square * (-1.0 / 720 + square / 40320))
    )
    which = near.astype(jnp.int32) & 3
    odd = (which & 1) == 1
    cos_abs = jnp.where(odd, sine, cosine)
    sin_abs = jnp.where(odd, cosine, sine)
    cos_value = jnp.where((which == 1) | (which == 2), -cos_abs, cos_abs)
    sin_value = jnp.where(which >= 2, -sin_abs, sin_abs)
    return cos_value, sin_value


def table_kernel(count_ref, inverse_ref, scale_ref, m_ref, t_ref, w_ref, coarse_ref):
    pair = pl.program_id(0)
    count, inverse, scale = count_ref[pair], inverse_ref[pair], scale_ref[pair]
    step = lax.broadcasted_iota(jnp.int32, (ROWS, LANE), 0).astype(F32)
    for g in range(m_ref.shape[0]):
        base = step * m_ref[g]
        fine_cos, fine_sin = turn(base, count, inverse)
        coarse_cos, coarse_sin = turn(base * 16.0, count, inverse)
        outer_cos, outer_sin = turn(base * float(TILE), count, inverse)
        w_ref[g, 0, 0:ROWS, :] = outer_cos * scale
        w_ref[g, 0, ROWS : 2 * ROWS, :] = outer_sin * scale
        coarse_ref[0:ROWS, :] = coarse_cos
        coarse_ref[ROWS : 2 * ROWS, :] = coarse_sin
        for a in range(TILE // ROWS):
            u_cos = coarse_ref[pl.ds(a, 1), :]
            u_sin = coarse_ref[pl.ds(ROWS + a, 1), :]
            rows = pl.ds(a * ROWS, ROWS)
            t_ref[g, 0, rows, 0:LANE] = (u_cos * fine_cos - u_sin * fine_sin).astype(BF16)
            t_ref[g, 0, rows, LANE : 2 * LANE] = (-(u_sin * fine_cos + u_cos * fine_sin)).astype(BF16)


def phase_tables(local_pairs, m_lanes):
    pairs = local_pairs.shape[0]
    groups = m_lanes.shape[0]
    count = (4 * local_pairs + 20).astype(F32)
    return pl.pallas_call(
        table_kernel,
        grid_spec=pltpu.PrefetchScalarGridSpec(
            num_scalar_prefetch=3,
            grid=(pairs,),
            in_specs=[pl.BlockSpec((groups, 1, LANE), lambda p, *_: (0, 0, 0))],
            out_specs=[
                pl.BlockSpec((groups, 1, TILE, 2 * LANE), lambda p, *_: (0, p, 0, 0)),
                pl.BlockSpec((groups, 1, 2 * ROWS, LANE), lambda p, *_: (0, p, 0, 0)),
            ],
            scratch_shapes=[pltpu.VMEM((2 * ROWS, LANE), F32)],
        ),
        out_shape=[
            jax.ShapeDtypeStruct((groups, pairs, TILE, 2 * LANE), BF16),
            jax.ShapeDtypeStruct((groups, pairs, 2 * ROWS, LANE), F32),
        ],
        compiler_params=params(32),
        cost_estimate=cost(10 * groups * pairs * TILE * 2 * LANE, 2 * groups * pairs * TILE * 2 * LANE),
        name="tables",
    )(count, 1.0 / count, 1.0 / jnp.sqrt(count), m_lanes)


def gather_kernel(slot_ref, room_ref, x_ref, o_ref, s_ref):
    sources, share, fields, cap, width = x_ref.shape
    s_ref[...] = jnp.zeros_like(s_ref)

    def unpack(source, carry):
        for l in range(share):
            for f in range(fields):
                value = x_ref[source, l, f].astype(F32)
                for h in range(2):
                    for t in range(TILE // LANE):
                        start = h * TILE + t * LANE
                        first = source * (cap * ROWS) + (h * 8 + f * share + l)
                        s_ref[t, pl.ds(first, cap, stride=ROWS), :] = value[:, start : start + LANE]
        return carry

    lax.fori_loop(0, sources, unpack, 0)
    lane = lax.broadcasted_iota(jnp.int32, (ROWS, LANE), 1)

    def place(block, carry):
        first = pl.multiple_of(slot_ref[block] * ROWS, ROWS)
        room = room_ref[block]
        out = pl.multiple_of(block * ROWS, ROWS)
        for t in range(TILE // LANE):
            value = s_ref[t, pl.ds(first, ROWS), :]
            value = jnp.where(lane < room - t * LANE, value, 0.0)
            o_ref[pl.ds(out, ROWS), t * LANE : (t + 1) * LANE] = value.astype(BF16)
        return carry

    lax.fori_loop(0, o_ref.shape[0] // ROWS, place, 0, unroll=8)


def gather_tiles(arrived, slots, room):
    sources, share, fields, cap, width = arrived.shape
    blocks = slots.shape[0]
    return pl.pallas_call(
        gather_kernel,
        grid_spec=pltpu.PrefetchScalarGridSpec(
            num_scalar_prefetch=2,
            grid=(1,),
            in_specs=[pl.BlockSpec(arrived.shape, lambda i, *_: (0, 0, 0, 0, 0))],
            out_specs=pl.BlockSpec((blocks * ROWS, TILE), lambda i, *_: (0, 0)),
            scratch_shapes=[pltpu.VMEM((TILE // LANE, sources * cap * ROWS, LANE), F32)],
        ),
        out_shape=jax.ShapeDtypeStruct((blocks * ROWS, TILE), BF16),
        compiler_params=params(58),
        cost_estimate=cost(8 * arrived.size, 2 * arrived.size + 2 * blocks * ROWS * TILE),
        name="place_tiles",
    )(slots, room, arrived)


def rows_kernel(blocks, lf, waves, pairs, x_ref, t_ref, w_ref, o_ref, f_ref):
    stage = pl.program_id(1)
    first = 0
    for k, count in enumerate(blocks):

        def one(first=first, count=count, k=k):
            for i in range(GROUP):
                begin = (first + i * count) * ROWS
                y = jnp.dot(
                    x_ref[begin : begin + count * ROWS, :], t_ref[0, i], preferred_element_type=F32
                )
                re = im = None
                for b in range(count):
                    y_re = y[b * ROWS : (b + 1) * ROWS, 0:LANE]
                    y_im = y[b * ROWS : (b + 1) * ROWS, LANE : 2 * LANE]
                    w_cos = w_ref[0, i, b : b + 1, :]
                    w_sin = w_ref[0, i, ROWS + b : ROWS + b + 1, :]
                    add_re = w_cos * y_re + w_sin * y_im
                    add_im = w_cos * y_im - w_sin * y_re
                    re = add_re if re is None else re + add_re
                    im = add_im if im is None else im + add_im
                j = k * GROUP + i
                for a, part in enumerate((re, im)):
                    part = part.astype(BF16).astype(F32)
                    north, south = part[0:8], part[8:16]
                    for s, total in enumerate((north + south, north - south)):
                        start = (s * 2 * lf + a * lf) * pairs + j
                        f_ref[pl.ds(start, lf, stride=pairs), :] = total[0:lf]

        pl.when(stage == k)(one)
        first += count * GROUP

    def pack():
        order = row_order(lf)
        piece = 16 if pairs % 16 == 0 else pairs
        for cg in range(-(-len(order) // waves)):
            for start in range(0, pairs, piece):
                items = []
                for p in range(cg * waves, (cg + 1) * waves):
                    if p < len(order):
                        kind, row = order[p]
                        items.append(f_ref[pl.ds((kind * 2 * lf + row) * pairs + start, piece), :])
                    else:
                        items.append(jnp.zeros((piece, LANE), F32))
                for d, value in enumerate(swap_blocks(items, LANE // waves)):
                    o_ref[
                        pl.ds(d * pairs + start, piece), cg * LANE : (cg + 1) * LANE
                    ] = value.astype(BF16)

    pl.when(stage == len(blocks) - 1)(pack)


def rows_to_waves(tiles, table, twist, blocks, lf, waves, chunk):
    pairs = table.shape[1]
    cgs = -(-4 * lf // waves)
    g0, ng = chunk[0], len(chunk)
    stages = len(blocks)
    return pl.pallas_call(
        functools.partial(rows_kernel, blocks, lf, waves, pairs),
        grid=(ng, stages),
        in_specs=[
            pl.BlockSpec(tiles.shape, lambda g, k: (0, 0)),
            pl.BlockSpec((1, GROUP, TILE, 2 * LANE), lambda g, k: (g0 + g, k, 0, 0)),
            pl.BlockSpec((1, GROUP, 2 * ROWS, LANE), lambda g, k: (g0 + g, k, 0, 0)),
        ],
        out_specs=pl.BlockSpec((waves * pairs, cgs * LANE), lambda g, k: (0, g)),
        out_shape=jax.ShapeDtypeStruct((waves * pairs, ng * cgs * LANE), BF16),
        scratch_shapes=[pltpu.VMEM((4 * lf * pairs, LANE), F32)],
        compiler_params=params(48),
        cost_estimate=cost(
            ng * 2 * tiles.size * 2 * LANE, 2 * tiles.size + ng * (2 * table[0].size + 4 * twist[0].size)
        ),
        name="rows_to_waves",
    )(tiles, table, twist)


def legendre_kernel(g0, per_group, waves, lf, total, own_ref, r_ref, p_ref, l_ref, *rest):
    s_ref, o_ref, d_ref, b_ref = rest[-4:]
    width = LANE // waves
    group, stage = pl.program_id(0), pl.program_id(1)
    many = l_ref.shape[0]
    order = row_order(lf)
    tiles = len(order) // 8
    rows = r_ref.shape[1]
    coefs = l_ref.shape[1]
    lanes = l_ref.shape[2] // LANE

    def begin():
        value = lax.dot_general(
            r_ref[...], p_ref[...], (((0,), (0,)), ((), ())), preferred_element_type=F32
        )
        for t in range(lanes):
            d_ref[t] = value[:, t * LANE : (t + 1) * LANE]
        if rows > len(order) * width:
            b_ref[...] = jnp.zeros_like(b_ref)

    pl.when(stage == 0)(begin)
    ordinal = lax.broadcasted_iota(jnp.int32, (8, coefs), 1)
    low_rows = lax.broadcasted_iota(jnp.int32, (8, coefs), 0) < 4

    for i in range(many):
        local = stage * many + i
        q = own_ref[(g0 + group) * per_group + local]

        def where_rows(w, tile, local=local):
            p = tile * 8
            start = p // waves * LANE + p % waves * width + 2 * local + w
            return pl.ds(start, 8, stride=width)

        picked = []
        for w in range(2):
            for tile in range(tiles):
                cut = where_rows(w, tile)
                picked.append(jnp.concatenate([d_ref[t, cut, :] for t in range(lanes)], axis=1))
        left = jnp.concatenate(picked, axis=0).astype(BF16)
        forward = lax.dot_general(
            left, l_ref[i], (((1,), (1,)), ((), ())), preferred_element_type=F32
        )
        split = total - q
        low = ordinal < split
        even = jnp.where(low, ordinal & 1, (ordinal - split) & 1) == 0
        chosen = [
            jnp.where(low, forward[t * 8 : t * 8 + 8], forward[(tiles + t) * 8 : (tiles + t) * 8 + 8])
            for t in range(tiles)
        ]
        head = jnp.where(even, chosen[0], chosen[1])
        tail = jnp.where(even, chosen[2], pltpu.roll(chosen[2], 4, 0))
        s_ref[i, 0:8, :] = head
        s_ref[i, 8:12, :] = tail[0:4]
        degree = jnp.where(low, q + ordinal, ordinal - 1).astype(F32)
        damping = 1.0 / (1.0 + 8.0 * degree * (degree + 1.0) / (total * total))
        head = head * damping
        tail = tail * damping
        tail = jnp.where(low_rows, tail, pltpu.roll(tail, 4, 0))
        parts = [head, jnp.where(even, head, -head), jnp.where(even | low_rows, tail, -tail)]
        back = jnp.concatenate(
            [jnp.where(low, x, 0.0) for x in parts] + [jnp.where(low, 0.0, x) for x in parts], axis=0
        ).astype(BF16)
        rebuilt = jnp.dot(back, l_ref[i], preferred_element_type=F32)
        for w in range(2):
            for tile in range(tiles):
                row = (w * tiles + tile) * 8
                cut = where_rows(w, tile)
                for t in range(lanes):
                    b_ref[t, cut, :] = rebuilt[row : row + 8, t * LANE : (t + 1) * LANE]

    def end():
        value = jnp.concatenate([b_ref[t].astype(BF16) for t in range(lanes)], axis=1)
        o_ref[...] = lax.dot_general(
            p_ref[...], value, (((1,), (1,)), ((), ())), preferred_element_type=F32
        ).astype(BF16)

    pl.when(stage == pl.num_programs(1) - 1)(end)


def legendre_both(received, places, legendre, own_sets, lf, waves, chunk, spectral):
    sets, coefs, pair_total = legendre.shape
    cgs = -(-4 * lf // waves)
    rows = cgs * LANE
    per_group = LANE // waves // 2
    many = 4
    stages = per_group // many
    g0, ng = chunk[0], len(chunk)
    block = lambda g, k, *_: ((g0 + g) * stages + k, 0, 0)
    in_specs = [
        pl.BlockSpec((pair_total, rows), lambda g, k, *_: (0, g)),
        pl.BlockSpec((pair_total, pair_total), lambda g, k, *_: (0, 0)),
        pl.BlockSpec((many, coefs, pair_total), block),
    ]
    operands = [own_sets, received, places, legendre]
    aliases = {}
    if spectral is not None:
        in_specs.append(pl.BlockSpec(memory_space=pl.ANY))
        operands.append(spectral)
        aliases = {4: 0}
    return pl.pallas_call(
        functools.partial(legendre_kernel, g0, per_group, waves, lf, coefs - 1),
        grid_spec=pltpu.PrefetchScalarGridSpec(
            num_scalar_prefetch=1,
            grid=(ng, stages),
            in_specs=in_specs,
            out_specs=[
                pl.BlockSpec((many, 2 * lf, coefs), block),
                pl.BlockSpec((pair_total, rows), lambda g, k, *_: (0, g)),
            ],
            scratch_shapes=[
                pltpu.VMEM((pair_total // LANE, rows, LANE), F32),
                pltpu.VMEM((pair_total // LANE, rows, LANE), F32),
            ],
        ),
        out_shape=[
            jax.ShapeDtypeStruct((sets, 2 * lf, coefs), F32),
            jax.ShapeDtypeStruct((pair_total, ng * rows), BF16),
        ],
        input_output_aliases=aliases,
        compiler_params=params(48),
        cost_estimate=cost(
            ng * per_group * 4 * 48 * coefs * pair_total, ng * per_group * 2 * coefs * pair_total
        ),
        name="legendre",
    )(*operands)


def unpack_kernel(order, lf, *refs):
    perm_ref, o_ref, g_ref = refs[-3:]
    parts = refs[:-3]
    sources, piece = parts[0].shape[0], parts[0].shape[1]
    width = LANE // sources
    cgs = -(-len(order) // sources)
    many = 4 * lf
    g = 0
    for ref in parts:
        for local in range(ref.shape[2] // (cgs * LANE)):
            for cg in range(cgs):
                start = (local * cgs + cg) * LANE
                items = [ref[s, :, start : start + LANE].astype(F32) for s in range(sources)]
                for d, value in enumerate(swap_blocks(items, width)):
                    p = cg * sources + d
                    if p < len(order):
                        kind, row = order[p]
                        g_ref[g, pl.ds(kind * 2 * lf + row, piece, stride=many), :] = value
            g += 1
    left = jnp.concatenate([g_ref[t].astype(BF16) for t in range(g)], axis=1)
    o_ref[...] = jnp.dot(left, perm_ref[...], preferred_element_type=F32).astype(BF16)


def unpack_rows(parts, perm, lf, waves):
    pairs = parts[0].shape[0] // waves
    piece = 16 if pairs % 16 == 0 else pairs
    total = perm.shape[0]
    shaped = [x.reshape(waves, pairs, x.shape[1]) for x in parts]
    size = sum(x.size for x in shaped)
    return pl.pallas_call(
        functools.partial(unpack_kernel, row_order(lf), lf),
        grid=(pairs // piece,),
        in_specs=[pl.BlockSpec((waves, piece, x.shape[2]), lambda j: (0, j, 0)) for x in shaped]
        + [pl.BlockSpec((total, total), lambda j: (0, 0))],
        out_specs=pl.BlockSpec((piece * 4 * lf, total), lambda j: (j, 0)),
        out_shape=jax.ShapeDtypeStruct((pairs * 4 * lf, total), BF16),
        scratch_shapes=[pltpu.VMEM((total // LANE, piece * 4 * lf, LANE), F32)],
        compiler_params=params(32),
        cost_estimate=cost(2 * size * total, 4 * size),
        name="unpack",
    )(*shaped, perm)


def body(grid_fields, diffusivity, tile_map, pair_order, m_order, legendre):
    waves = lax.axis_size("wave")
    groups = lax.axis_size("lev")
    me = lax.axis_index("wave")
    levels, fields, slots, width = grid_fields.shape
    cap = slots // waves
    share = levels // groups
    lf = share * fields
    pair_total = pair_order.shape[0]
    pairs = pair_total // waves
    set_total = m_order.shape[0]
    sets = set_total // waves
    waves_total = 2 * set_total
    lane_groups = waves_total // LANE
    run = LANE // waves

    outgoing = diffuse(grid_fields, diffusivity, waves, groups)
    outgoing = outgoing.reshape(waves * groups, share, fields, cap, width)
    arrived = lax.all_to_all(outgoing, ("wave", "lev"), 0, 0, tiled=True)

    local_pairs = lax.dynamic_slice_in_dim(pair_order, me * pairs, pairs)
    picks = jnp.stack([m_order, waves_total - 1 - m_order], axis=1)
    m_lanes = picks.reshape(waves, lane_groups, run).transpose(1, 0, 2)
    m_lanes = m_lanes.reshape(lane_groups, 1, LANE).astype(F32)
    table, twist = phase_tables(local_pairs, m_lanes)

    stages = pairs // GROUP
    blocks = []
    for k in range(stages):
        largest = waves * (k * GROUP + GROUP - 1) + waves - 1
        blocks.append(min(BLK, -(-(4 * largest + 20) // TILE)))
    pair_at = [k * GROUP + i for k in range(stages) for i in range(GROUP) for _ in range(blocks[k])]
    block_at = [b for k in range(stages) for i in range(GROUP) for b in range(blocks[k])]
    pair_at = jnp.asarray(pair_at, jnp.int32)
    block_at = jnp.asarray(block_at, jnp.int32)
    pair_ids = jnp.take(local_pairs, pair_at)
    wanted = pair_ids * BLK + block_at
    room = 4 * pair_ids + 20 - block_at * TILE
    catalog = tile_map.reshape(waves, groups, waves, cap)
    own = lax.dynamic_index_in_dim(catalog, me, axis=2, keepdims=False).reshape(-1)
    slot_ids = jnp.arange(own.shape[0], dtype=jnp.int32)
    found = jnp.where(own[None, :] == wanted[:, None], slot_ids[None, :], 0)
    slot_of = jnp.max(found, axis=1)

    tiles = gather_tiles(arrived, slot_of, room)

    places = (pair_order[:, None] == jnp.arange(pair_total, dtype=jnp.int32)[None, :]).astype(BF16)
    own_sets = lax.dynamic_slice_in_dim(m_order, me * sets, sets)
    lane = jnp.arange(waves_total, dtype=jnp.int32)
    spot = lane // LANE * run + lane % run
    column = spot % 2 * set_total + lane % LANE // run * sets + spot // 2
    perm = (column[:, None] == lane[None, :]).astype(BF16)

    received = []
    for chunk in CHUNKS:
        sent = rows_to_waves(tiles, table, twist, tuple(blocks), lf, waves, chunk)
        received.append(lax.all_to_all(sent, "wave", 0, 0, tiled=True))
    spectral = None
    returned = []
    for chunk, part in zip(CHUNKS, received):
        spectral, back = legendre_both(
            part, places, legendre, own_sets, lf, waves, chunk, spectral
        )
        returned.append(lax.all_to_all(back, "wave", 0, 0, tiled=True))
    fourier_out = unpack_rows(returned, perm, lf, waves)
    spectral = spectral.reshape(sets, 2, fields, share, legendre.shape[1])
    fourier_out = fourier_out.reshape(pairs, 2, 2, fields, share, waves_total)
    return spectral, fourier_out


def solution(mesh):
    return jax.shard_map(
        body,
        mesh=mesh,
        in_specs=(
            P(None, None, ("wave", "lev"), None),
            P(None, ("wave", "lev"), None),
            P(),
            P(),
            P(),
            P("wave", None, None),
        ),
        out_specs=(P("wave", None, None, "lev", None), P("wave", None, None, None, "lev", None)),
        check_vma=False,
    )
```

profile of v0, /device:TPU:0, one launch (start us, length us, event | category | flops | bytes accessed | tf_op | source)
XLA Modules:
  0.0 266.3 jit_solution(3954554439179385391)
XLA Ops:
  0.6 0.0 copy-start.1
  0.6 2.8 %copy-done.1 = f32[8,3,128,512]{3,2,1,0:T(8,128)S(1)} copy-done((f32[8,3,128,512]{3,2,1,0:T(8,128)S(1)}, f32[8,3,128,512]{3,2,1,0:T(8,128)}, u32[]{:S(2)}) %copy-start.1) | copy-done | bytes 6291480
  3.4 0.0 copy-start.5
  3.4 1.2 copy-done.5
  4.6 4.5 %diffuse.1 = bf16[8,4,2,3,16,512]{5,4,3,2,1,0:T(8,128)(2,1)} custom-call(f32[8,3,8,16,512]{4,3,2,1,0:T(8,128)S(1)} %bitcast.8, bf16[7,8,16,512]{3,2,1,0:T(8,128)(2,1)S(1)} %bitcast.10), custom_call_target="tpu_custom_call" | custom-call | flops 62914560 | bytes 10354688 | tf_op jit(solution)/shard_map/diffuse/pallas_call | solution.py:96
  9.1 0.0 copy-start.8
  9.1 0.0 copy-start.9
  9.1 0.0 copy-start.10
  9.1 0.0 copy-start.13
  9.1 7.3 %all-to-all-start = ((bf16[32,2,3,16,512]{4,3,2,1,0:T(8,128)(2,1)}), bf16[32,2,3,16,512]{4,3,2,1,0:T(8,128)(2,1)S(1)}, u32[]{:S(2)}, u32[]{:S(2)}) async-start(bf16[32,2,3,16,512]{4,3,2,1,0:T(8,128)(2,1)} %bitcast.2), calls=%async_computation | async-start | bytes 6291456 | tf_op jit(solution)/shard_map/all_to_all | solution.py:493
  16.5 0.0 copy-done.8
  16.5 0.1 reshape.127
  16.6 0.1 dynamic-slice_reduce_fusion
  16.6 0.1 eq.45
  16.7 0.0 copy-done.9
  16.8 0.1 copy.16
  16.9 0.1 convert_element_type.20
  17.0 0.1 convert_element_type.22.m_ref
  17.1 0.0 copy-done.10
  17.1 0.1 fusion.29
  17.2 0.0 copy-done.13
  17.2 0.0 copy-start.11
  17.2 0.0 copy-start.12
  17.2 3.8 %gather_fusion = s32[520]{0:T(1024)S(1)} fusion(s32[80]{0:T(128)S(1)} %get-tuple-element.15, s32[1024]{0:T(1024)S(1)} %pad_clamp_fusion), kind=kCustom, calls=%fused_computation | custom fusion | bytes 6240 | tf_op jit(solution)/shard_map/jit(_take)/gather | solution.py:510
  21.1 50.7 %tables.1 = (bf16[5,80,256,256]{3,2,1,0:T(8,128)(2,1)}, f32[5,80,32,128]{3,2,1,0:T(8,128)S(1)}) custom-call(f32[80]{0:T(128)S(1)} %add_convert_fusion.1.count_ref, f32[80]{0:T(128)S(1)} %broadcast_divide_fusion.inverse_ref, f32[80]{0:T(128)S(1)} %get-tuple-element.14.scale_ref, f32[5,1,128]{2,1,0:T(1,128)S(1)} %convert_element_type.22.m_ref), custom_call_target="tpu_custom_call" | custom-call | flops 262144000 | bytes 52428800 | tf_op jit(solution)/shard_map/tables/pallas_call | solution.py:157
  71.8 0.0 copy-start
  71.8 2.7 %copy-done = f32[5,80,32,128]{3,2,1,0:T(8,128)} copy-done((f32[5,80,32,128]{3,2,1,0:T(8,128)}, f32[5,80,32,128]{3,2,1,0:T(8,128)S(1)}, u32[]{:S(2)}) %copy-start) | copy-done | bytes 6553624
  74.5 0.0 copy-done.11
  74.5 0.0 copy-done.12
  74.5 0.6 add_add_fusion
  75.1 0.9 select_reduce_fusion.slot_ref
  76.0 10.6 %all-to-all-done.x_ref = bf16[32,2,3,16,512]{4,3,2,1,0:T(8,128)(2,1)S(1)} async-done(((bf16[32,2,3,16,512]{4,3,2,1,0:T(8,128)(2,1)}), bf16[32,2,3,16,512]{4,3,2,1,0:T(8,128)(2,1)S(1)}, u32[]{:S(2)}, u32[]{:S(2)}) %all-to-all-start) | async-done | bytes 3145760 | tf_op jit(solution)/shard_map/all_to_all | solution.py:493
  86.6 0.0 copy-start.6
  86.6 1.6 copy-done.6
  88.2 9.5 %place_tiles.1.x_ref = bf16[8320,256]{1,0:T(8,128)(2,1)} custom-call(s32[520]{0:T(1024)} %select_reduce_fusion.slot_ref, s32[520]{0:T(1024)} %get-tuple-element.16.room_ref, bf16[32,2,3,16,512]{4,3,2,1,0:T(8,128)(2,1)} %copy-done.6), custom_call_target="tpu_custom_call" | custom-call | flops 12582912 | bytes 7405568 | tf_op jit(solution)/shard_map/place_tiles/pallas_call | solution.py:213
  97.7 50.9 %rows_to_waves.1 = bf16[640,1920]{1,0:T(8,128)(2,1)} custom-call(bf16[8320,256]{1,0:T(8,128)(2,1)} %place_tiles.1.x_ref, bf16[5,80,256,256]{3,2,1,0:T(8,128)(2,1)} %get-tuple-element.6.t_ref, f32[5,80,32,128]{3,2,1,0:T(8,128)} %copy-done), custom_call_target="tpu_custom_call" | custom-call | flops 5452595200 | bytes 63242240 | tf_op jit(solution)/shard_map/rows_to_waves/pallas_call | solution.py:286
  148.6 4.1 %all-to-all-start.1 = ((bf16[8,80,1920]{2,1,0:T(8,128)(2,1)}), bf16[8,80,1920]{2,1,0:T(8,128)(2,1)S(1)}, u32[]{:S(2)}, u32[]{:S(2)}) async-start(bf16[8,80,1920]{2,1,0:T(8,128)(2,1)} %bitcast.4), calls=%async_computation.1 | async-start | bytes 4915200 | tf_op jit(solution)/shard_map/all_to_all | solution.py:531
  152.7 0.1 dynamic_slice.10.own_ref
  152.8 23.0 %copy.18.l_ref = bf16[40,641,640]{2,1,0:T(8,128)(2,1)} copy(bf16[40,641,640]{2,0,1:T(8,128)(2,1)} %param.13) | data formatting | bytes 65638400 | tf_op args[5]
  175.8 0.2 fusion.p_ref
  176.0 7.2 %all-to-all-done.1 = bf16[8,80,1920]{2,1,0:T(8,128)(2,1)S(1)} async-done(((bf16[8,80,1920]{2,1,0:T(8,128)(2,1)}), bf16[8,80,1920]{2,1,0:T(8,128)(2,1)S(1)}, u32[]{:S(2)}, u32[]{:S(2)}) %all-to-all-start.1) | async-done | bytes 2457632 | tf_op jit(solution)/shard_map/all_to_all | solution.py:531
  183.2 0.0 copy-start.7
  183.2 1.4 copy-done.7
  184.7 31.4 %legendre.1 = (f32[40,12,641]{2,1,0:T(8,128)S(1)}, bf16[640,1920]{1,0:T(8,128)(2,1)S(1)}) custom-call(s32[40]{0:T(128)S(1)} %dynamic_slice.10.own_ref, bf16[640,1920]{1,0:T(8,128)(2,1)} %bitcast.11, bf16[640,640]{1,0:T(8,128)(2,1)S(1)} %fusion.p_ref, bf16[40,641,640]{2,1,0:T(8,128)(2,1)} %copy.18.l_ref), custom_call_target="tpu_custom_call" | custom-call | flops 3150643200 | bytes 32819200 | tf_op jit(solution)/shard_map/legendre/pallas_call | solution.py:404
  216.0 0.0 copy-start.2
  216.0 1.4 copy-done.2
  217.5 0.0 copy-start.4
  217.5 1.3 copy-done.4
  218.7 3.8 %all-to-all-start.2 = ((bf16[8,80,1920]{2,1,0:T(8,128)(2,1)}), bf16[8,80,1920]{2,1,0:T(8,128)(2,1)S(1)}, u32[]{:S(2)}, u32[]{:S(2)}) async-start(bf16[8,80,1920]{2,1,0:T(8,128)(2,1)} %bitcast.9), calls=%async_computation.2 | async-start | bytes 4915200 | tf_op jit(solution)/shard_map/all_to_all | solution.py:538
  222.6 0.2 fusion.1.refs_1_
  222.8 2.4 copy.19
  225.2 1.9 copy.20
  227.1 25.8 %all-to-all-done.2.refs_0_ = bf16[8,80,1920]{2,1,0:T(8,128)(2,1)S(1)} async-done(((bf16[8,80,1920]{2,1,0:T(8,128)(2,1)}), bf16[8,80,1920]{2,1,0:T(8,128)(2,1)S(1)}, u32[]{:S(2)}, u32[]{:S(2)}) %all-to-all-start.2) | async-done | bytes 2457632 | tf_op jit(solution)/shard_map/all_to_all | solution.py:538
  252.8 5.9 %unpack.1 = bf16[1920,640]{1,0:T(8,128)(2,1)S(1)} custom-call(bf16[8,80,1920]{2,1,0:T(8,128)(2,1)S(1)} %all-to-all-done.2.refs_0_, bf16[640,640]{1,0:T(8,128)(2,1)S(1)} %fusion.1.refs_1_), custom_call_target="tpu_custom_call" | custom-call | flops 1572864000 | bytes 4915200 | tf_op jit(solution)/shard_map/unpack/pallas_call | solution.py:461
  258.7 0.0 copy-start.3
  258.7 1.5 copy-done.3
  260.2 6.1 %reshape.132 = bf16[80,2,2,3,2,640]{5,4,3,2,1,0:T(2,128)(2,1)} reshape(bf16[1920,640]{1,0:T(8,128)(2,1)} %copy-done.3) | data formatting | bytes 4915200 | tf_op jit(solution)/shard_map/reshape | solution.py:541
  (9 shorter events, 0.1 us)
Async XLA Ops:
  0.6 2.8 %copy-start.1 = (f32[8,3,128,512]{3,2,1,0:T(8,128)S(1)}, f32[8,3,128,512]{3,2,1,0:T(8,128)}, u32[]{:S(2)}) copy-start(f32[8,3,128,512]{3,2,1,0:T(8,128)} %param.8) | copy-start | bytes 18874372
  3.4 1.2 copy-start.5
  9.1 7.3 %copy-start.8 = (s32[4096]{0:T(1024)S(1)}, s32[4096]{0:T(1024)}, u32[]{:S(2)}) copy-start(s32[4096]{0:T(1024)} %param.10) | copy-start | bytes 49156
  9.1 7.6 %copy-start.9 = (s32[320]{0:T(512)S(1)}, s32[320]{0:T(512)}, u32[]{:S(2)}) copy-start(s32[320]{0:T(512)} %param.12) | copy-start | bytes 3844
  9.1 8.0 %copy-start.10 = (s32[640]{0:T(1024)S(1)}, s32[640]{0:T(1024)}, u32[]{:S(2)}) copy-start(s32[640]{0:T(1024)} %param.11) | copy-start | bytes 7684
  9.1 8.1 %copy-start.13 = (s32[520]{0:T(1024)S(1)}, s32[520]{0:T(1024)}, u32[]{:S(2)}) copy-start(s32[520]{0:T(1024)} %constant.137) | copy-start | bytes 6244
  9.1 77.5 %all-to-all-start = ((bf16[32,2,3,16,512]{4,3,2,1,0:T(8,128)(2,1)}), bf16[32,2,3,16,512]{4,3,2,1,0:T(8,128)(2,1)S(1)}, u32[]{:S(2)}, u32[]{:S(2)}) async-start(bf16[32,2,3,16,512]{4,3,2,1,0:T(8,128)(2,1)} %bitcast.2), calls=%async_computation | async-start | bytes 6291456 | tf_op jit(solution)/shard_map/all_to_all | solution.py:493
  17.2 57.3 %copy-start.11 = (s32[520]{0:T(1024)S(1)}, s32[520]{0:T(1024)}, u32[]{:S(2)}) copy-start(s32[520]{0:T(1024)} %constant.136) | copy-start | bytes 6244
  17.2 57.3 %copy-start.12 = (s32[520]{0:T(1024)S(1)}, s32[520]{0:T(1024)}, u32[]{:S(2)}) copy-start(s32[520]{0:T(1024)} %constant.126.clone) | copy-start | bytes 6244
  71.8 2.7 %copy-start = (f32[5,80,32,128]{3,2,1,0:T(8,128)}, f32[5,80,32,128]{3,2,1,0:T(8,128)S(1)}, u32[]{:S(2)}) copy-start(f32[5,80,32,128]{3,2,1,0:T(8,128)S(1)} %get-tuple-element.7.w_ref) | copy-start | bytes 19660804
  86.6 1.6 copy-start.6
  148.6 34.6 %all-to-all-start.1 = ((bf16[8,80,1920]{2,1,0:T(8,128)(2,1)}), bf16[8,80,1920]{2,1,0:T(8,128)(2,1)S(1)}, u32[]{:S(2)}, u32[]{:S(2)}) async-start(bf16[8,80,1920]{2,1,0:T(8,128)(2,1)} %bitcast.4), calls=%async_computation.1 | async-start | bytes 4915200 | tf_op jit(solution)/shard_map/all_to_all | solution.py:531
  183.2 1.4 copy-start.7
  216.0 1.4 copy-start.2
  217.5 1.3 copy-start.4
  218.7 34.1 %all-to-all-start.2 = ((bf16[8,80,1920]{2,1,0:T(8,128)(2,1)}), bf16[8,80,1920]{2,1,0:T(8,128)(2,1)S(1)}, u32[]{:S(2)}, u32[]{:S(2)}) async-start(bf16[8,80,1920]{2,1,0:T(8,128)(2,1)} %bitcast.9), calls=%async_computation.2 | async-start | bytes 4915200 | tf_op jit(solution)/shard_map/all_to_all | solution.py:538
  258.7 1.5 copy-start.3
where the time goes:
time: 268 us; the launch traced here: 266 us
  Pallas kernels  153 us (57%)
  local copies, waits for them, and re-layouts  51.8 us (19%)
  waiting for transfers between devices  43.5 us (16%)
  starting transfers between devices  15.2 us (6%)
    pallas_call x1, Pallas kernels, rows_to_waves(): pl.pallas_call(functools.partial(rows_kernel, blocks, lf, waves, pairs),...  50.9 us
    pallas_call x1, Pallas kernels, phase_tables(): pl.pallas_call(table_kernel, grid_spec=pltpu.PrefetchScalarGridSpec(num_s...  50.7 us
    unnamed x30, local copies, waits for them, and re-layouts  38.8 us
    pallas_call x1, Pallas kernels, legendre_both(): pl.pallas_call(functools.partial(legendre_kernel, g0, per_group, waves, l...  31.4 us
    all_to_all x1, waiting for transfers between devices, body(): returned.append(lax.all_to_all(back, 'wave', 0, 0, tiled=True))  25.8 us
    all_to_all x1, waiting for transfers between devices, body(): arrived = lax.all_to_all(outgoing, ('wave', 'lev'), 0, 0, tiled=True)  10.6 us
    pallas_call x1, Pallas kernels, gather_tiles(): pl.pallas_call(gather_kernel, grid_spec=pltpu.PrefetchScalarGridSpec(num_...  9.47 us
    all_to_all x1, starting transfers between devices, body(): arrived = lax.all_to_all(outgoing, ('wave', 'lev'), 0, 0, tiled=True)  7.3 us
  transfers between devices with their start and end apart: 3, of which 3 were waited for; matrix products, arithmetic and copies ran while one was open for 13% of the time, Pallas kernels for 19%

commit v1 on v0

--- a/solution.py
+++ b/solution.py
@@ -9,13 +9,18 @@
 
 TILE = 256
 BLK = 11
+SPAN = 17
 LANE = 128
 ROWS = 16
-GROUP = 8
 F32 = jnp.float32
 BF16 = jnp.bfloat16
 MIB = 1024 * 1024
-CHUNKS = ((0, 1, 2, 3, 4),)
+STEPS = (4, 8, 11)
+CHUNKS = (2, 3)
+
+
+def group_of(pairs):
+    return 16 if pairs % 16 == 0 else 8
 
 
 def params(mib):
@@ -102,7 +107,7 @@
         ],
         out_specs=pl.BlockSpec((1, groups, share, fields, cap, width), lambda w: (w, 0, 0, 0, 0, 0)),
         out_shape=jax.ShapeDtypeStruct((waves, groups, share, fields, cap, width), BF16),
-        compiler_params=params(32),
+        compiler_params=params(60),
         cost_estimate=cost(40 * x.size, 6 * x.size + 2 * a.size),
         name="diffuse",
     )(x, a)
@@ -129,57 +134,66 @@
     return cos_value, sin_value
 
 
-def table_kernel(count_ref, inverse_ref, scale_ref, m_ref, t_ref, w_ref, coarse_ref):
-    pair = pl.program_id(0)
-    count, inverse, scale = count_ref[pair], inverse_ref[pair], scale_ref[pair]
+def table_kernel(chunks, count_ref, inverse_ref, scale_ref, m_ref, *refs):
+    group = refs[0].shape[1]
+    coarse_ref = refs[-1]
     step = lax.broadcasted_iota(jnp.int32, (ROWS, LANE), 0).astype(F32)
-    for g in range(m_ref.shape[0]):
-        base = step * m_ref[g]
-        fine_cos, fine_sin = turn(base, count, inverse)
-        coarse_cos, coarse_sin = turn(base * 16.0, count, inverse)
-        outer_cos, outer_sin = turn(base * float(TILE), count, inverse)
-        w_ref[g, 0, 0:ROWS, :] = outer_cos * scale
-        w_ref[g, 0, ROWS : 2 * ROWS, :] = outer_sin * scale
-        coarse_ref[0:ROWS, :] = coarse_cos
-        coarse_ref[ROWS : 2 * ROWS, :] = coarse_sin
-        for a in range(TILE // ROWS):
-            u_cos = coarse_ref[pl.ds(a, 1), :]
-            u_sin = coarse_ref[pl.ds(ROWS + a, 1), :]
-            rows = pl.ds(a * ROWS, ROWS)
-            t_ref[g, 0, rows, 0:LANE] = (u_cos * fine_cos - u_sin * fine_sin).astype(BF16)
-            t_ref[g, 0, rows, LANE : 2 * LANE] = (-(u_sin * fine_cos + u_cos * fine_sin)).astype(BF16)
-
-
-def phase_tables(local_pairs, m_lanes):
+    spots = [(c, g) for c, size in enumerate(chunks) for g in range(size)]
+
+    def one(i, carry):
+        pair = pl.program_id(0) * group + i
+        count, inverse, scale = count_ref[pair], inverse_ref[pair], scale_ref[pair]
+        for at, (c, g) in enumerate(spots):
+            t_ref, w_ref = refs[2 * c], refs[2 * c + 1]
+            base = step * m_ref[at]
+            fine_cos, fine_sin = turn(base, count, inverse)
+            coarse_cos, coarse_sin = turn(base * 16.0, count, inverse)
+            outer_cos, outer_sin = turn(base * float(TILE), count, inverse)
+            w_ref[g, i, 0:ROWS, :] = outer_cos * scale
+            w_ref[g, i, ROWS : 2 * ROWS, :] = outer_sin * scale
+            coarse_ref[at, 0:ROWS, :] = coarse_cos
+            coarse_ref[at, ROWS : 2 * ROWS, :] = coarse_sin
+            for a in range(TILE // ROWS):
+                u_cos = coarse_ref[at, pl.ds(a, 1), :]
+                u_sin = coarse_ref[at, pl.ds(ROWS + a, 1), :]
+                rows = pl.ds(a * ROWS, ROWS)
+                t_ref[g, i, rows, 0:LANE] = (u_cos * fine_cos - u_sin * fine_sin).astype(BF16)
+                t_ref[g, i, rows, LANE : 2 * LANE] = (-(u_sin * fine_cos + u_cos * fine_sin)).astype(BF16)
+        return carry
+
+    lax.fori_loop(0, group, one, 0)
+
+
+def phase_tables(local_pairs, m_lanes, chunks):
     pairs = local_pairs.shape[0]
     groups = m_lanes.shape[0]
+    group = group_of(pairs)
     count = (4 * local_pairs + 20).astype(F32)
+    specs, shapes = [], []
+    for ng in chunks:
+        specs.append(pl.BlockSpec((ng, group, TILE, 2 * LANE), lambda p, *_: (0, p, 0, 0)))
+        specs.append(pl.BlockSpec((ng, group, 2 * ROWS, LANE), lambda p, *_: (0, p, 0, 0)))
+        shapes.append(jax.ShapeDtypeStruct((ng, pairs, TILE, 2 * LANE), BF16))
+        shapes.append(jax.ShapeDtypeStruct((ng, pairs, 2 * ROWS, LANE), F32))
     return pl.pallas_call(
-        table_kernel,
+        functools.partial(table_kernel, chunks),
         grid_spec=pltpu.PrefetchScalarGridSpec(
             num_scalar_prefetch=3,
-            grid=(pairs,),
+            grid=(pairs // group,),
             in_specs=[pl.BlockSpec((groups, 1, LANE), lambda p, *_: (0, 0, 0))],
-            out_specs=[
-                pl.BlockSpec((groups, 1, TILE, 2 * LANE), lambda p, *_: (0, p, 0, 0)),
-                pl.BlockSpec((groups, 1, 2 * ROWS, LANE), lambda p, *_: (0, p, 0, 0)),
-            ],
-            scratch_shapes=[pltpu.VMEM((2 * ROWS, LANE), F32)],
+            out_specs=specs,
+            scratch_shapes=[pltpu.VMEM((groups, 2 * ROWS, LANE), F32)],
         ),
-        out_shape=[
-            jax.ShapeDtypeStruct((groups, pairs, TILE, 2 * LANE), BF16),
-            jax.ShapeDtypeStruct((groups, pairs, 2 * ROWS, LANE), F32),
-        ],
-        compiler_params=params(32),
+        out_shape=shapes,
+        compiler_params=params(48),
         cost_estimate=cost(10 * groups * pairs * TILE * 2 * LANE, 2 * groups * pairs * TILE * 2 * LANE),
         name="tables",
     )(count, 1.0 / count, 1.0 / jnp.sqrt(count), m_lanes)
 
 
-def gather_kernel(slot_ref, room_ref, x_ref, o_ref, s_ref):
+def gather_kernel(group, slot_ref, room_ref, x_ref, ahead_ref, o_ref, s_ref):
+    del ahead_ref
     sources, share, fields, cap, width = x_ref.shape
-    s_ref[...] = jnp.zeros_like(s_ref)
-
     def unpack(source, carry):
         for l in range(share):
             for f in range(fields):
@@ -187,116 +201,136 @@
                 for h in range(2):
                     for t in range(TILE // LANE):
                         start = h * TILE + t * LANE
-                        first = source * (cap * ROWS) + (h * 8 + f * share + l)
-                        s_ref[t, pl.ds(first, cap, stride=ROWS), :] = value[:, start : start + LANE]
+                        first = source * (cap * SPAN) + (h * 8 + f * share + l)
+                        s_ref[t, pl.ds(first, cap, stride=SPAN), :] = value[:, start : start + LANE]
         return carry
 
     lax.fori_loop(0, sources, unpack, 0)
     lane = lax.broadcasted_iota(jnp.int32, (ROWS, LANE), 1)
 
-    def place(block, carry):
-        first = pl.multiple_of(slot_ref[block] * ROWS, ROWS)
-        room = room_ref[block]
-        out = pl.multiple_of(block * ROWS, ROWS)
-        for t in range(TILE // LANE):
-            value = s_ref[t, pl.ds(first, ROWS), :]
-            value = jnp.where(lane < room - t * LANE, value, 0.0)
-            o_ref[pl.ds(out, ROWS), t * LANE : (t + 1) * LANE] = value.astype(BF16)
+    def place(batch, carry):
+        for i in range(group):
+            block = batch * group + i
+            first, room = slot_ref[block] * SPAN, room_ref[block]
+            rows = pl.ds(pl.multiple_of(block * ROWS, ROWS), ROWS)
+            for t in range(TILE // LANE):
+                value = s_ref[t, pl.ds(first, ROWS), :]
+                value = jnp.where(lane < room - t * LANE, value, 0.0)
+                o_ref[rows, t * LANE : (t + 1) * LANE] = value.astype(BF16)
         return carry
 
-    lax.fori_loop(0, o_ref.shape[0] // ROWS, place, 0, unroll=8)
-
-
-def gather_tiles(arrived, slots, room):
+    lax.fori_loop(0, o_ref.shape[0] // (ROWS * group), place, 0)
+
+
+def gather_tiles(arrived, slots, room, ahead):
     sources, share, fields, cap, width = arrived.shape
     blocks = slots.shape[0]
     return pl.pallas_call(
-        gather_kernel,
+        functools.partial(gather_kernel, 16 if blocks % 16 == 0 else 8),
         grid_spec=pltpu.PrefetchScalarGridSpec(
             num_scalar_prefetch=2,
             grid=(1,),
-            in_specs=[pl.BlockSpec(arrived.shape, lambda i, *_: (0, 0, 0, 0, 0))],
+            in_specs=[
+                pl.BlockSpec(arrived.shape, lambda i, *_: (0, 0, 0, 0, 0)),
+                pl.BlockSpec(memory_space=pl.ANY),
+            ],
             out_specs=pl.BlockSpec((blocks * ROWS, TILE), lambda i, *_: (0, 0)),
-            scratch_shapes=[pltpu.VMEM((TILE // LANE, sources * cap * ROWS, LANE), F32)],
+            scratch_shapes=[pltpu.VMEM((TILE // LANE, sources * cap * SPAN, LANE), F32)],
         ),
         out_shape=jax.ShapeDtypeStruct((blocks * ROWS, TILE), BF16),
         compiler_params=params(58),
         cost_estimate=cost(8 * arrived.size, 2 * arrived.size + 2 * blocks * ROWS * TILE),
         name="place_tiles",
-    )(slots, room, arrived)
+    )(slots, room, arrived, ahead)
 
 
 def rows_kernel(blocks, lf, waves, pairs, x_ref, t_ref, w_ref, o_ref, f_ref):
-    stage = pl.program_id(1)
+    stage = pl.program_id(0)
+    many, group = t_ref.shape[:2]
+    order = row_order(lf)
+    cgs = -(-len(order) // waves)
     first = 0
-    for k, count in enumerate(blocks):
-
-        def one(first=first, count=count, k=k):
-            for i in range(GROUP):
-                begin = (first + i * count) * ROWS
-                y = jnp.dot(
-                    x_ref[begin : begin + count * ROWS, :], t_ref[0, i], preferred_element_type=F32
-                )
-                re = im = None
-                for b in range(count):
-                    y_re = y[b * ROWS : (b + 1) * ROWS, 0:LANE]
-                    y_im = y[b * ROWS : (b + 1) * ROWS, LANE : 2 * LANE]
-                    w_cos = w_ref[0, i, b : b + 1, :]
-                    w_sin = w_ref[0, i, ROWS + b : ROWS + b + 1, :]
-                    add_re = w_cos * y_re + w_sin * y_im
-                    add_im = w_cos * y_im - w_sin * y_re
-                    re = add_re if re is None else re + add_re
-                    im = add_im if im is None else im + add_im
-                j = k * GROUP + i
-                for a, part in enumerate((re, im)):
-                    part = part.astype(BF16).astype(F32)
-                    north, south = part[0:8], part[8:16]
-                    for s, total in enumerate((north + south, north - south)):
-                        start = (s * 2 * lf + a * lf) * pairs + j
-                        f_ref[pl.ds(start, lf, stride=pairs), :] = total[0:lf]
-
-        pl.when(stage == k)(one)
-        first += count * GROUP
+    begin = 0
+    while begin < len(blocks):
+        count = blocks[begin]
+        end = begin + blocks.count(count)
+
+        def bucket(first=first, begin=begin, count=count):
+            base = first + (stage - begin) * (group * count)
+
+            def one(g, carry):
+                for i in range(group):
+                    top = pl.multiple_of((base + i * count) * ROWS, ROWS)
+                    rows = pl.ds(top, count * ROWS)
+                    y = jnp.dot(x_ref[rows, :], t_ref[g, i], preferred_element_type=F32)
+                    re = im = None
+                    for b in range(count):
+                        y_re = y[b * ROWS : (b + 1) * ROWS, 0:LANE]
+                        y_im = y[b * ROWS : (b + 1) * ROWS, LANE : 2 * LANE]
+                        w_cos = w_ref[g, i, b : b + 1, :]
+                        w_sin = w_ref[g, i, ROWS + b : ROWS + b + 1, :]
+                        add_re = w_cos * y_re + w_sin * y_im
+                        add_im = w_cos * y_im - w_sin * y_re
+                        re = add_re if re is None else re + add_re
+                        im = add_im if im is None else im + add_im
+                    j = stage * group + i
+                    for a, part in enumerate((re, im)):
+                        part = part.astype(BF16).astype(F32)
+                        north, south = part[0:8], part[8:16]
+                        for s, total in enumerate((north + south, north - south)):
+                            start = (s * 2 * lf + a * lf) * pairs + j
+                            f_ref[g, pl.ds(start, lf, stride=pairs), :] = total[0:lf]
+                return carry
+
+            lax.fori_loop(0, many, one, 0)
+
+        pl.when((stage >= begin) & (stage < end))(bucket)
+        first += count * group * (end - begin)
+        begin = end
+
+    piece = 16 if pairs % 16 == 0 else pairs
 
     def pack():
-        order = row_order(lf)
-        piece = 16 if pairs % 16 == 0 else pairs
-        for cg in range(-(-len(order) // waves)):
-            for start in range(0, pairs, piece):
+        def one(step, carry):
+            g, start = step // (pairs // piece), step % (pairs // piece) * piece
+            for cg in range(cgs):
                 items = []
                 for p in range(cg * waves, (cg + 1) * waves):
                     if p < len(order):
                         kind, row = order[p]
-                        items.append(f_ref[pl.ds((kind * 2 * lf + row) * pairs + start, piece), :])
+                        top = pl.multiple_of((kind * 2 * lf + row) * pairs + start, 8)
+                        items.append(f_ref[g, pl.ds(top, piece), :])
                     else:
                         items.append(jnp.zeros((piece, LANE), F32))
+                lane = pl.multiple_of((g * cgs + cg) * LANE, LANE)
                 for d, value in enumerate(swap_blocks(items, LANE // waves)):
-                    o_ref[
-                        pl.ds(d * pairs + start, piece), cg * LANE : (cg + 1) * LANE
-                    ] = value.astype(BF16)
+                    top = pl.multiple_of(d * pairs + start, piece)
+                    o_ref[pl.ds(top, piece), pl.ds(lane, LANE)] = value.astype(BF16)
+            return carry
+
+        lax.fori_loop(0, many * (pairs // piece), one, 0, unroll=pairs // piece)
 
     pl.when(stage == len(blocks) - 1)(pack)
 
 
-def rows_to_waves(tiles, table, twist, blocks, lf, waves, chunk):
-    pairs = table.shape[1]
+def rows_to_waves(tiles, table, twist, blocks, lf, waves):
+    ng, pairs = table.shape[:2]
+    group = group_of(pairs)
     cgs = -(-4 * lf // waves)
-    g0, ng = chunk[0], len(chunk)
-    stages = len(blocks)
     return pl.pallas_call(
         functools.partial(rows_kernel, blocks, lf, waves, pairs),
-        grid=(ng, stages),
+        grid=(len(blocks),),
         in_specs=[
-            pl.BlockSpec(tiles.shape, lambda g, k: (0, 0)),
-            pl.BlockSpec((1, GROUP, TILE, 2 * LANE), lambda g, k: (g0 + g, k, 0, 0)),
-            pl.BlockSpec((1, GROUP, 2 * ROWS, LANE), lambda g, k: (g0 + g, k, 0, 0)),
+            pl.BlockSpec(tiles.shape, lambda k: (0, 0)),
+            pl.BlockSpec((ng, group, TILE, 2 * LANE), lambda k: (0, k, 0, 0)),
+            pl.BlockSpec((ng, group, 2 * ROWS, LANE), lambda k: (0, k, 0, 0)),
         ],
-        out_specs=pl.BlockSpec((waves * pairs, cgs * LANE), lambda g, k: (0, g)),
+        out_specs=pl.BlockSpec((waves * pairs, ng * cgs * LANE), lambda k: (0, 0)),
         out_shape=jax.ShapeDtypeStruct((waves * pairs, ng * cgs * LANE), BF16),
-        scratch_shapes=[pltpu.VMEM((4 * lf * pairs, LANE), F32)],
-        compiler_params=params(48),
+        scratch_shapes=[pltpu.VMEM((ng, 4 * lf * pairs, LANE), F32)],
+        compiler_params=params(56),
         cost_estimate=cost(
-            ng * 2 * tiles.size * 2 * LANE, 2 * tiles.size + ng * (2 * table[0].size + 4 * twist[0].size)
+            ng * 2 * tiles.size * 2 * LANE, 2 * tiles.size + 2 * table.size + 4 * twist.size
         ),
         name="rows_to_waves",
     )(tiles, table, twist)
@@ -388,7 +422,7 @@
     per_group = LANE // waves // 2
     many = 4
     stages = per_group // many
-    g0, ng = chunk[0], len(chunk)
+    g0, ng = chunk
     block = lambda g, k, *_: ((g0 + g) * stages + k, 0, 0)
     in_specs = [
         pl.BlockSpec((pair_total, rows), lambda g, k, *_: (0, g)),
@@ -433,23 +467,23 @@
     perm_ref, o_ref, g_ref = refs[-3:]
     parts = refs[:-3]
     sources, piece = parts[0].shape[0], parts[0].shape[1]
-    width = LANE // sources
     cgs = -(-len(order) // sources)
-    many = 4 * lf
     g = 0
     for ref in parts:
         for local in range(ref.shape[2] // (cgs * LANE)):
             for cg in range(cgs):
                 start = (local * cgs + cg) * LANE
-                items = [ref[s, :, start : start + LANE].astype(F32) for s in range(sources)]
-                for d, value in enumerate(swap_blocks(items, width)):
+                items = [ref[s, :, start : start + LANE] for s in range(sources)]
+                for d, value in enumerate(swap_blocks(items, LANE // sources)):
                     p = cg * sources + d
                     if p < len(order):
                         kind, row = order[p]
-                        g_ref[g, pl.ds(kind * 2 * lf + row, piece, stride=many), :] = value
+                        top = (kind * 2 * lf + row) * piece
+                        g_ref[g, top : top + piece, :] = value
             g += 1
-    left = jnp.concatenate([g_ref[t].astype(BF16) for t in range(g)], axis=1)
-    o_ref[...] = jnp.dot(left, perm_ref[...], preferred_element_type=F32).astype(BF16)
+    left = jnp.concatenate([g_ref[t] for t in range(g)], axis=1)
+    value = jnp.dot(left, perm_ref[...], preferred_element_type=F32).astype(BF16)
+    o_ref[...] = value.reshape(o_ref.shape)
 
 
 def unpack_rows(parts, perm, lf, waves):
@@ -462,10 +496,12 @@
         functools.partial(unpack_kernel, row_order(lf), lf),
         grid=(pairs // piece,),
         in_specs=[pl.BlockSpec((waves, piece, x.shape[2]), lambda j: (0, j, 0)) for x in shaped]
-        + [pl.BlockSpec((total, total), lambda j: (0, 0))],
-        out_specs=pl.BlockSpec((piece * 4 * lf, total), lambda j: (j, 0)),
-        out_shape=jax.ShapeDtypeStruct((pairs * 4 * lf, total), BF16),
-        scratch_shapes=[pltpu.VMEM((total // LANE, piece * 4 * lf, LANE), F32)],
+        + [
+            pl.BlockSpec((total, total), lambda j: (0, 0)),
+        ],
+        out_specs=pl.BlockSpec((4 * lf, piece, total), lambda j: (0, j, 0)),
+        out_shape=jax.ShapeDtypeStruct((4 * lf, pairs, total), BF16),
+        scratch_shapes=[pltpu.VMEM((total // LANE, piece * 4 * lf, LANE), BF16)],
         compiler_params=params(32),
         cost_estimate=cost(2 * size * total, 4 * size),
         name="unpack",
@@ -496,15 +532,18 @@
     picks = jnp.stack([m_order, waves_total - 1 - m_order], axis=1)
     m_lanes = picks.reshape(waves, lane_groups, run).transpose(1, 0, 2)
     m_lanes = m_lanes.reshape(lane_groups, 1, LANE).astype(F32)
-    table, twist = phase_tables(local_pairs, m_lanes)
-
-    stages = pairs // GROUP
+    chunks = CHUNKS if sum(CHUNKS) == lane_groups else (lane_groups,)
+    tables = phase_tables(local_pairs, m_lanes, chunks)
+
+    group = group_of(pairs)
+    stages = pairs // group
     blocks = []
     for k in range(stages):
-        largest = waves * (k * GROUP + GROUP - 1) + waves - 1
-        blocks.append(min(BLK, -(-(4 * largest + 20) // TILE)))
-    pair_at = [k * GROUP + i for k in range(stages) for i in range(GROUP) for _ in range(blocks[k])]
-    block_at = [b for k in range(stages) for i in range(GROUP) for b in range(blocks[k])]
+        largest = waves * (k * group + group - 1) + waves - 1
+        least = min(BLK, -(-(4 * largest + 20) // TILE))
+        blocks.append(min(x for x in STEPS if x >= least))
+    pair_at = [k * group + i for k in range(stages) for i in range(group) for _ in range(blocks[k])]
+    block_at = [b for k in range(stages) for i in range(group) for b in range(blocks[k])]
     pair_at = jnp.asarray(pair_at, jnp.int32)
     block_at = jnp.asarray(block_at, jnp.int32)
     pair_ids = jnp.take(local_pairs, pair_at)
@@ -516,7 +555,7 @@
     found = jnp.where(own[None, :] == wanted[:, None], slot_ids[None, :], 0)
     slot_of = jnp.max(found, axis=1)
 
-    tiles = gather_tiles(arrived, slot_of, room)
+    tiles = gather_tiles(arrived, slot_of, room, legendre)
 
     places = (pair_order[:, None] == jnp.arange(pair_total, dtype=jnp.int32)[None, :]).astype(BF16)
     own_sets = lax.dynamic_slice_in_dim(m_order, me * sets, sets)
@@ -526,19 +565,23 @@
     perm = (column[:, None] == lane[None, :]).astype(BF16)
 
     received = []
-    for chunk in CHUNKS:
-        sent = rows_to_waves(tiles, table, twist, tuple(blocks), lf, waves, chunk)
+    for c in range(len(chunks)):
+        sent = rows_to_waves(
+            tiles, tables[2 * c], tables[2 * c + 1], tuple(blocks), lf, waves
+        )
         received.append(lax.all_to_all(sent, "wave", 0, 0, tiled=True))
     spectral = None
     returned = []
-    for chunk, part in zip(CHUNKS, received):
+    begin = 0
+    for ng, part in zip(chunks, received):
         spectral, back = legendre_both(
-            part, places, legendre, own_sets, lf, waves, chunk, spectral
+            part, places, legendre, own_sets, lf, waves, (begin, ng), spectral
         )
+        begin += ng
         returned.append(lax.all_to_all(back, "wave", 0, 0, tiled=True))
     fourier_out = unpack_rows(returned, perm, lf, waves)
     spectral = spectral.reshape(sets, 2, fields, share, legendre.shape[1])
-    fourier_out = fourier_out.reshape(pairs, 2, 2, fields, share, waves_total)
+    fourier_out = fourier_out.transpose(1, 0, 2).reshape(pairs, 2, 2, fields, share, waves_total)
     return spectral, fourier_out
 
 

time: 268 us -> 222 us (0.83)
  Pallas kernels: 153 us -> 129 us
  waiting for transfers between devices: 43.5 us -> 23.3 us
  local copies, waits for them, and re-layouts: 51.8 us -> 40.9 us
  starting transfers between devices: 15.2 us -> 24 us
    pallas_call x2, Pallas kernels: 60.2 us -> 42.8 us  [the longest x1 35 us: phase_tables(): pl.pallas_call(functools.partial(table_kernel, chunks), grid_spec=pltpu.P...]
    pallas_call x1 -> x2, Pallas kernels: 50.9 us -> 38 us  [rows_to_waves(): pl.pallas_call(functools.partial(rows_kernel, blocks, lf, waves, pairs),...]
    all_to_all x1 -> x2, waiting for transfers between devices: 25.8 us -> 16.1 us  [body(): returned.append(lax.all_to_all(back, 'wave', 0, 0, tiled=True))]
    all_to_all x1, waiting for transfers between devices: 10.6 us -> 3.67 us  [body(): arrived = lax.all_to_all(outgoing, ('wave', 'lev'), 0, 0, tiled=True)]
    reshape x1 -> x0, local copies, waits for them, and re-layouts: 6.11 us -> none  [body(): fourier_out = fourier_out.reshape(pairs, 2, 2, fields, share, waves_total)]
    all_to_all x1 -> x2, starting transfers between devices: 3.8 us -> 8.32 us  [body(): returned.append(lax.all_to_all(back, 'wave', 0, 0, tiled=True))]
    all_to_all x1 -> x2, starting transfers between devices: 4.06 us -> 8.34 us  [body(): received.append(lax.all_to_all(sent, 'wave', 0, 0, tiled=True))]
    unnamed x30 -> x29, local copies, waits for them, and re-layouts: 38.8 us -> 34.9 us
  transfers between devices with their start and end apart: 3 -> 5, of which waited for: 3 -> 3; matrix products, arithmetic and copies ran while one was open for 13% -> 15% of each run, Pallas kernels for 19% -> 41%
where the time goes in v1:
time: 222 us; the launch traced here: 221 us
  Pallas kernels  129 us (58%)
  local copies, waits for them, and re-layouts  40.9 us (18%)
  starting transfers between devices  24 us (11%)
  waiting for transfers between devices  23.3 us (10%)
  other arithmetic  2.99 us (1%)
    pallas_call x2, Pallas kernels, rows_to_waves(): pl.pallas_call(functools.partial(rows_kernel, blocks, lf, waves, pairs),...  38 us
    pallas_call x1, Pallas kernels, phase_tables(): pl.pallas_call(functools.partial(table_kernel, chunks), grid_spec=pltpu.P...  35 us
    unnamed x29, local copies, waits for them, and re-layouts  34.9 us
    pallas_call x2, Pallas kernels, legendre_both(): pl.pallas_call(functools.partial(legendre_kernel, g0, per_group, waves, l...  34 us
    all_to_all x2, waiting for transfers between devices, body(): returned.append(lax.all_to_all(back, 'wave', 0, 0, tiled=True))  16.1 us
    all_to_all x2, starting transfers between devices, body(): received.append(lax.all_to_all(sent, 'wave', 0, 0, tiled=True))  8.34 us
    all_to_all x2, starting transfers between devices, body(): returned.append(lax.all_to_all(back, 'wave', 0, 0, tiled=True))  8.32 us
    pallas_call x1, Pallas kernels, gather_tiles(): pl.pallas_call(functools.partial(gather_kernel, 16 if blocks % 16 == 0 el...  7.81 us
  transfers between devices with their start and end apart: 5, of which 3 were waited for; matrix products, arithmetic and copies ran while one was open for 15% of the time, Pallas kernels for 41%

profile of v1, /device:TPU:0, one launch (start us, length us, event | category | flops | bytes accessed | tf_op | source)
XLA Modules:
  0.0 220.9 jit_solution(2513455035182190893)
XLA Ops:
  0.6 7.6 %diffuse.1 = bf16[8,4,2,3,16,512]{5,4,3,2,1,0:T(8,128)(2,1)} custom-call(f32[8,3,8,16,512]{4,3,2,1,0:T(8,128)} %bitcast.19, bf16[7,8,16,512]{3,2,1,0:T(8,128)(2,1)} %bitcast.23), custom_call_target="tpu_custom_call" | custom-call | flops 62914560 | bytes 10354688 | tf_op jit(solution)/shard_map/diffuse/pallas_call | solution.py:101
  8.2 0.0 copy-start.7
  8.2 7.3 %all-to-all-start = ((bf16[32,2,3,16,512]{4,3,2,1,0:T(8,128)(2,1)}), bf16[32,2,3,16,512]{4,3,2,1,0:T(8,128)(2,1)S(1)}, u32[]{:S(2)}, u32[]{:S(2)}) async-start(bf16[32,2,3,16,512]{4,3,2,1,0:T(8,128)(2,1)} %bitcast.18), calls=%async_computation | async-start | bytes 6291456 | tf_op jit(solution)/shard_map/all_to_all | solution.py:529
  15.5 0.0 copy-done.7
  15.6 0.1 reshape.133
  15.7 0.1 dynamic-slice_reduce_fusion
  15.7 0.1 eq.45
  15.8 0.0 copy-start.8
  15.8 0.0 copy-start.9
  15.8 0.0 copy-start.12
  15.8 23.1 %copy.23.ahead_ref.l_ref = bf16[40,641,640]{2,1,0:T(8,128)(2,1)} copy(bf16[40,641,640]{2,0,1:T(8,128)(2,1)} %param.13) | data formatting | bytes 65638400 | tf_op args[5]
  38.9 0.0 copy-done.8
  39.0 0.1 copy.24
  39.1 0.1 convert_element_type.20
  39.3 0.1 convert_element_type.22.m_ref
  39.4 0.0 copy-done.9
  39.4 0.1 fusion.29
  39.4 0.0 copy-done.12
  39.5 0.0 copy-start.10
  39.5 0.0 copy-start.11
  39.5 4.5 %gather_fusion = s32[672]{0:T(1024)S(1)} fusion(s32[80]{0:T(128)S(1)} %get-tuple-element.25, s32[1024]{0:T(1024)S(1)} %pad_clamp_fusion), kind=kCustom, calls=%fused_computation | custom fusion | bytes 8064 | tf_op jit(solution)/shard_map/jit(_take)/gather | solution.py:549
  44.0 35.0 %tables.1 = (bf16[2,80,256,256]{3,2,1,0:T(8,128)(2,1)}, f32[2,80,32,128]{3,2,1,0:T(8,128)S(1)}, bf16[3,80,256,256]{3,2,1,0:T(8,128)(2,1)}, f32[3,80,32,128]{3,2,1,0:T(8,128)}) custom-call(f32[80]{0:T(128)S(1)} %add_convert_fusion.1.count_ref, f32[80]{0:T(128)S(1)} %broadcast_divide_fusion.inverse_ref, f32[80]{0:T(128)S(1)} %get-tuple-element.24.scale_ref, ...), custom_call_target="tpu_custom_call" | custom-call | flops 262144000 | bytes 52428800 | tf_op jit(solution)/shard_map/tables/pallas_call | solution.py:178
  79.0 0.0 copy-start.2
  79.0 1.5 copy-done.2
  80.5 0.0 copy-done.10
  80.5 0.0 copy-done.11
  80.5 0.6 add_add_fusion
  81.1 1.0 select_reduce_fusion.slot_ref
  82.0 3.7 %all-to-all-done.x_ref = bf16[32,2,3,16,512]{4,3,2,1,0:T(8,128)(2,1)S(1)} async-done(((bf16[32,2,3,16,512]{4,3,2,1,0:T(8,128)(2,1)}), bf16[32,2,3,16,512]{4,3,2,1,0:T(8,128)(2,1)S(1)}, u32[]{:S(2)}, u32[]{:S(2)}) %all-to-all-start) | async-done | bytes 3145760 | tf_op jit(solution)/shard_map/all_to_all | solution.py:529
  85.7 0.0 copy-start.6
  85.7 1.8 copy-done.6
  87.5 7.8 %place_tiles.1.x_ref = bf16[10752,256]{1,0:T(8,128)(2,1)} custom-call(s32[672]{0:T(1024)} %select_reduce_fusion.slot_ref, s32[672]{0:T(1024)} %get-tuple-element.26.room_ref, bf16[32,2,3,16,512]{4,3,2,1,0:T(8,128)(2,1)} %copy-done.6, bf16[40,641,640]{2,1,0:T(8,128)(2,1)} %copy.23.ahead_ref.l_ref), custom_call_target="tpu_custom_call" | custom-call | flops 12582912 | bytes 8650752 | tf_op jit(solution)/shard_map/place_tiles/pallas_call | solution.py:228
  95.3 16.3 %rows_to_waves.3 = bf16[640,768]{1,0:T(8,128)(2,1)} custom-call(bf16[10752,256]{1,0:T(8,128)(2,1)} %place_tiles.1.x_ref, bf16[2,80,256,256]{3,2,1,0:T(8,128)(2,1)} %get-tuple-element.12.t_ref, f32[2,80,32,128]{3,2,1,0:T(8,128)} %copy-done.2), custom_call_target="tpu_custom_call" | custom-call | flops 2818572288 | bytes 29097984 | tf_op jit(solution)/shard_map/rows_to_waves/pallas_call | solution.py:320
  111.6 4.0 %all-to-all-start.2 = ((bf16[8,80,768]{2,1,0:T(8,128)(2,1)}), bf16[8,80,768]{2,1,0:T(8,128)(2,1)S(1)}, u32[]{:S(2)}, u32[]{:S(2)}) async-start(bf16[8,80,768]{2,1,0:T(8,128)(2,1)} %bitcast.22), calls=%async_computation.2 | async-start | bytes 1966080 | tf_op jit(solution)/shard_map/all_to_all | solution.py:572
  115.6 21.8 %rows_to_waves.2 = bf16[640,1152]{1,0:T(8,128)(2,1)} custom-call(bf16[10752,256]{1,0:T(8,128)(2,1)} %place_tiles.1.x_ref, bf16[3,80,256,256]{3,2,1,0:T(8,128)(2,1)} %get-tuple-element.10.t_ref, f32[3,80,32,128]{3,2,1,0:T(8,128)} %get-tuple-element.11.w_ref), custom_call_target="tpu_custom_call" | custom-call | flops 4227858432 | bytes 40894464 | tf_op jit(solution)/shard_map/rows_to_waves/pallas_call | solution.py:320
  137.4 0.0 all-to-all-done.2
  137.4 0.0 copy-start
  137.4 4.3 %all-to-all-start.1 = ((bf16[8,80,1152]{2,1,0:T(8,128)(2,1)}), bf16[8,80,1152]{2,1,0:T(8,128)(2,1)}, u32[]{:S(2)}, u32[]{:S(2)}) async-start(bf16[8,80,1152]{2,1,0:T(8,128)(2,1)} %bitcast.21), calls=%async_computation.1 | async-start | bytes 2949120 | tf_op jit(solution)/shard_map/all_to_all | solution.py:572
  141.7 0.1 dynamic_slice.10.own_ref
  141.8 0.2 fusion.p_ref
  142.0 0.0 copy-done
  142.0 0.0 copy-start.1
  142.0 1.2 copy-done.1
  143.2 14.1 %legendre.2 = (f32[40,12,641]{2,1,0:T(8,128)S(1)}, bf16[640,768]{1,0:T(8,128)(2,1)S(1)}) custom-call(s32[40]{0:T(128)S(1)} %dynamic_slice.10.own_ref, bf16[640,768]{1,0:T(8,128)(2,1)S(1)} %bitcast.14, bf16[640,640]{1,0:T(8,128)(2,1)S(1)} %fusion.p_ref, bf16[40,641,640]{2,1,0:T(8,128)(2,1)} %copy.23.ahead_ref.l_ref), custom_call_target="tpu_custom_call" | custom-call | flops 1260257280 | bytes 13127680 | tf_op jit(solution)/shard_map/legendre/pallas_call | solution.py:438
  157.3 0.0 copy-start.4
  157.3 0.9 copy-done.4
  158.2 3.5 %all-to-all-done.1 = bf16[8,80,1152]{2,1,0:T(8,128)(2,1)} async-done(((bf16[8,80,1152]{2,1,0:T(8,128)(2,1)}), bf16[8,80,1152]{2,1,0:T(8,128)(2,1)}, u32[]{:S(2)}, u32[]{:S(2)}) %all-to-all-start.1) | async-done | bytes 1474592 | tf_op jit(solution)/shard_map/all_to_all | solution.py:572
  161.7 4.4 %all-to-all-start.3 = ((bf16[8,80,768]{2,1,0:T(8,128)(2,1)}), bf16[8,80,768]{2,1,0:T(8,128)(2,1)}, u32[]{:S(2)}, u32[]{:S(2)}) async-start(bf16[8,80,768]{2,1,0:T(8,128)(2,1)} %bitcast.17), calls=%async_computation.3 | async-start | bytes 1966080 | tf_op jit(solution)/shard_map/all_to_all | solution.py:581
  166.1 19.9 %legendre.3 = (f32[40,12,641]{2,1,0:T(8,128)S(1)}, bf16[640,1152]{1,0:T(8,128)(2,1)S(1)}) custom-call(s32[40]{0:T(128)S(1)} %dynamic_slice.10.own_ref, bf16[640,1152]{1,0:T(8,128)(2,1)} %bitcast.5.r_ref, bf16[640,640]{1,0:T(8,128)(2,1)S(1)} %fusion.p_ref, bf16[40,641,640]{2,1,0:T(8,128)(2,1)} %copy.23.ahead_ref.l_ref, ...), custom_call_target="tpu_custom_call", output_to_operand_aliasing={{0}: (4, {})} | custom-call | flops 1890385920 | bytes 19691520 | tf_op jit(solution)/shard_map/legendre/pallas_call | solution.py:438
  186.0 0.0 copy-start.3
  186.0 1.1 copy-done.3
  187.1 0.0 all-to-all-done.3.refs_0_
  187.1 3.9 %all-to-all-start.4 = ((bf16[8,80,1152]{2,1,0:T(8,128)(2,1)}), bf16[8,80,1152]{2,1,0:T(8,128)(2,1)S(1)}, u32[]{:S(2)}, u32[]{:S(2)}) async-start(bf16[8,80,1152]{2,1,0:T(8,128)(2,1)} %bitcast.16), calls=%async_computation.4 | async-start | bytes 2949120 | tf_op jit(solution)/shard_map/all_to_all | solution.py:581
  191.0 1.1 fusion.1.refs_2_
  192.1 0.9 copy.28
  193.0 0.0 copy-start.5
  193.0 1.9 copy.29
  194.9 16.1 %all-to-all-done.4.refs_1_ = bf16[8,80,1152]{2,1,0:T(8,128)(2,1)S(1)} async-done(((bf16[8,80,1152]{2,1,0:T(8,128)(2,1)}), bf16[8,80,1152]{2,1,0:T(8,128)(2,1)S(1)}, u32[]{:S(2)}, u32[]{:S(2)}) %all-to-all-start.4) | async-done | bytes 1474592 | tf_op jit(solution)/shard_map/all_to_all | solution.py:581
  211.0 0.0 copy-done.5
  211.0 6.5 %unpack.1 = bf16[24,80,640]{2,1,0:T(8,128)(2,1)S(1)} custom-call(bf16[8,80,768]{2,1,0:T(8,128)(2,1)} %all-to-all-done.3.refs_0_, bf16[8,80,1152]{2,1,0:T(8,128)(2,1)S(1)} %all-to-all-done.4.refs_1_, bf16[640,640]{1,0:T(8,128)(2,1)S(1)} %copy-done.5), custom_call_target="tpu_custom_call" | custom-call | flops 1572864000 | bytes 4915200 | tf_op jit(solution)/shard_map/unpack/pallas_call | solution.py:495
  217.5 3.3 %copy.30 = bf16[80,2,2,3,2,640]{5,4,3,2,1,0:T(2,128)(2,1)} copy(bf16[80,2,2,3,2,640]{5,0,4,3,2,1:T(8,128)(2,1)S(1)} %bitcast.15) | data formatting | bytes 4915200
  (9 shorter events, 0.1 us)
Async XLA Ops:
  8.2 7.3 %copy-start.7 = (s32[4096]{0:T(1024)S(1)}, s32[4096]{0:T(1024)}, u32[]{:S(2)}) copy-start(s32[4096]{0:T(1024)} %param.10) | copy-start | bytes 49156
  8.2 77.5 %all-to-all-start = ((bf16[32,2,3,16,512]{4,3,2,1,0:T(8,128)(2,1)}), bf16[32,2,3,16,512]{4,3,2,1,0:T(8,128)(2,1)S(1)}, u32[]{:S(2)}, u32[]{:S(2)}) async-start(bf16[32,2,3,16,512]{4,3,2,1,0:T(8,128)(2,1)} %bitcast.18), calls=%async_computation | async-start | bytes 6291456 | tf_op jit(solution)/shard_map/all_to_all | solution.py:529
  15.8 23.1 %copy-start.8 = (s32[320]{0:T(512)S(1)}, s32[320]{0:T(512)}, u32[]{:S(2)}) copy-start(s32[320]{0:T(512)} %param.12) | copy-start | bytes 3844
  15.8 23.5 %copy-start.9 = (s32[640]{0:T(1024)S(1)}, s32[640]{0:T(1024)}, u32[]{:S(2)}) copy-start(s32[640]{0:T(1024)} %param.11) | copy-start | bytes 7684
  15.8 23.6 %copy-start.12 = (s32[672]{0:T(1024)S(1)}, s32[672]{0:T(1024)}, u32[]{:S(2)}) copy-start(s32[672]{0:T(1024)} %constant.137) | copy-start | bytes 8068
  39.5 41.0 %copy-start.10 = (s32[672]{0:T(1024)S(1)}, s32[672]{0:T(1024)}, u32[]{:S(2)}) copy-start(s32[672]{0:T(1024)} %constant.136) | copy-start | bytes 8068
  39.5 41.0 %copy-start.11 = (s32[672]{0:T(1024)S(1)}, s32[672]{0:T(1024)}, u32[]{:S(2)}) copy-start(s32[672]{0:T(1024)} %constant.126.clone) | copy-start | bytes 8068
  79.0 1.5 copy-start.2
  85.7 1.8 copy-start.6
  111.6 25.8 %all-to-all-start.2 = ((bf16[8,80,768]{2,1,0:T(8,128)(2,1)}), bf16[8,80,768]{2,1,0:T(8,128)(2,1)S(1)}, u32[]{:S(2)}, u32[]{:S(2)}) async-start(bf16[8,80,768]{2,1,0:T(8,128)(2,1)} %bitcast.22), calls=%async_computation.2 | async-start | bytes 1966080 | tf_op jit(solution)/shard_map/all_to_all | solution.py:572
  137.4 4.6 %copy-start = (bf16[8,80,768]{2,1,0:T(8,128)(2,1)}, bf16[8,80,768]{2,1,0:T(8,128)(2,1)S(1)}, u32[]{:S(2)}) copy-start(bf16[8,80,768]{2,1,0:T(8,128)(2,1)S(1)} %all-to-all-done.2) | copy-start | bytes 2949124
  137.4 24.3 %all-to-all-start.1 = ((bf16[8,80,1152]{2,1,0:T(8,128)(2,1)}), bf16[8,80,1152]{2,1,0:T(8,128)(2,1)}, u32[]{:S(2)}, u32[]{:S(2)}) async-start(bf16[8,80,1152]{2,1,0:T(8,128)(2,1)} %bitcast.21), calls=%async_computation.1 | async-start | bytes 2949120 | tf_op jit(solution)/shard_map/all_to_all | solution.py:572
  142.0 1.2 copy-start.1
  157.3 0.9 copy-start.4
  161.7 25.4 %all-to-all-start.3 = ((bf16[8,80,768]{2,1,0:T(8,128)(2,1)}), bf16[8,80,768]{2,1,0:T(8,128)(2,1)}, u32[]{:S(2)}, u32[]{:S(2)}) async-start(bf16[8,80,768]{2,1,0:T(8,128)(2,1)} %bitcast.17), calls=%async_computation.3 | async-start | bytes 1966080 | tf_op jit(solution)/shard_map/all_to_all | solution.py:581
  186.0 1.1 copy-start.3
  187.1 23.9 %all-to-all-start.4 = ((bf16[8,80,1152]{2,1,0:T(8,128)(2,1)}), bf16[8,80,1152]{2,1,0:T(8,128)(2,1)S(1)}, u32[]{:S(2)}, u32[]{:S(2)}) async-start(bf16[8,80,1152]{2,1,0:T(8,128)(2,1)} %bitcast.16), calls=%async_computation.4 | async-start | bytes 2949120 | tf_op jit(solution)/shard_map/all_to_all | solution.py:581
  193.0 18.0 %copy-start.5 = (bf16[640,640]{1,0:T(8,128)(2,1)S(1)}, bf16[640,640]{1,0:T(8,128)(2,1)}, u32[]{:S(2)}) copy-start(bf16[640,640]{1,0:T(8,128)(2,1)} %fusion.1.refs_2_) | copy-start | bytes 2457604

commit v2 on v1

--- a/solution.py
+++ b/solution.py
@@ -15,7 +15,6 @@
 F32 = jnp.float32
 BF16 = jnp.bfloat16
 MIB = 1024 * 1024
-STEPS = (4, 8, 11)
 CHUNKS = (2, 3)
 
 
@@ -173,8 +172,8 @@
     for ng in chunks:
         specs.append(pl.BlockSpec((ng, group, TILE, 2 * LANE), lambda p, *_: (0, p, 0, 0)))
         specs.append(pl.BlockSpec((ng, group, 2 * ROWS, LANE), lambda p, *_: (0, p, 0, 0)))
-        shapes.append(jax.ShapeDtypeStruct((ng, pairs, TILE, 2 * LANE), BF16))
-        shapes.append(jax.ShapeDtypeStruct((ng, pairs, 2 * ROWS, LANE), F32))
+        shapes.append(pltpu.HBM((ng, pairs, TILE, 2 * LANE), BF16))
+        shapes.append(pltpu.HBM((ng, pairs, 2 * ROWS, LANE), F32))
     return pl.pallas_call(
         functools.partial(table_kernel, chunks),
         grid_spec=pltpu.PrefetchScalarGridSpec(
@@ -191,9 +190,9 @@
     )(count, 1.0 / count, 1.0 / jnp.sqrt(count), m_lanes)
 
 
-def gather_kernel(group, slot_ref, room_ref, x_ref, ahead_ref, o_ref, s_ref):
-    del ahead_ref
+def place_tiles(blocks, group, slot_ref, room_ref, x_ref, o_ref, s_ref):
     sources, share, fields, cap, width = x_ref.shape
+
     def unpack(source, carry):
         for l in range(share):
             for f in range(fields):
@@ -208,60 +207,52 @@
     lax.fori_loop(0, sources, unpack, 0)
     lane = lax.broadcasted_iota(jnp.int32, (ROWS, LANE), 1)
 
-    def place(batch, carry):
-        for i in range(group):
-            block = batch * group + i
-            first, room = slot_ref[block] * SPAN, room_ref[block]
-            rows = pl.ds(pl.multiple_of(block * ROWS, ROWS), ROWS)
-            for t in range(TILE // LANE):
-                value = s_ref[t, pl.ds(first, ROWS), :]
-                value = jnp.where(lane < room - t * LANE, value, 0.0)
-                o_ref[rows, t * LANE : (t + 1) * LANE] = value.astype(BF16)
-        return carry
-
-    lax.fori_loop(0, o_ref.shape[0] // (ROWS * group), place, 0)
-
-
-def gather_tiles(arrived, slots, room, ahead):
-    sources, share, fields, cap, width = arrived.shape
-    blocks = slots.shape[0]
-    return pl.pallas_call(
-        functools.partial(gather_kernel, 16 if blocks % 16 == 0 else 8),
-        grid_spec=pltpu.PrefetchScalarGridSpec(
-            num_scalar_prefetch=2,
-            grid=(1,),
-            in_specs=[
-                pl.BlockSpec(arrived.shape, lambda i, *_: (0, 0, 0, 0, 0)),
-                pl.BlockSpec(memory_space=pl.ANY),
-            ],
-            out_specs=pl.BlockSpec((blocks * ROWS, TILE), lambda i, *_: (0, 0)),
-            scratch_shapes=[pltpu.VMEM((TILE // LANE, sources * cap * SPAN, LANE), F32)],
-        ),
-        out_shape=jax.ShapeDtypeStruct((blocks * ROWS, TILE), BF16),
-        compiler_params=params(58),
-        cost_estimate=cost(8 * arrived.size, 2 * arrived.size + 2 * blocks * ROWS * TILE),
-        name="place_tiles",
-    )(slots, room, arrived, ahead)
-
-
-def rows_kernel(blocks, lf, waves, pairs, x_ref, t_ref, w_ref, o_ref, f_ref):
-    stage = pl.program_id(0)
+    seen = 0
+    for k, count in enumerate(blocks):
+
+        def place(step, carry, seen=seen):
+            for i in range(group):
+                local = step * group + i
+                first, room = slot_ref[seen + local] * SPAN, room_ref[seen + local]
+                rows = pl.ds(pl.multiple_of((seen + local) * ROWS, ROWS), ROWS)
+                for t in range(TILE // LANE):
+                    value = s_ref[t, pl.ds(first, ROWS), :]
+                    value = jnp.where(lane < room - t * LANE, value, 0.0)
+                    o_ref[rows, t * LANE : (t + 1) * LANE] = value.astype(BF16)
+            return carry
+
+        lax.fori_loop(0, count, place, 0)
+        seen += count * group
+
+
+def rows_stage(blocks, lf, waves, pairs, stage, x_ref, t_ref, w_ref, o_ref, f_ref):
     many, group = t_ref.shape[:2]
     order = row_order(lf)
     cgs = -(-len(order) // waves)
-    first = 0
-    begin = 0
-    while begin < len(blocks):
-        count = blocks[begin]
-        end = begin + blocks.count(count)
-
-        def bucket(first=first, begin=begin, count=count):
-            base = first + (stage - begin) * (group * count)
-
+
+    def pack(start, g, carry):
+        for cg in range(cgs):
+            items = []
+            for p in range(cg * waves, (cg + 1) * waves):
+                if p < len(order):
+                    kind, row = order[p]
+                    top = (kind * 2 * lf + row) * (group + 1)
+                    items.append(f_ref[g, top : top + group, :])
+                else:
+                    items.append(jnp.zeros((group, LANE), F32))
+            lane = pl.multiple_of((g * cgs + cg) * LANE, LANE)
+            for d, value in enumerate(swap_blocks(items, LANE // waves)):
+                top = d * pairs + start
+                o_ref[top : top + group, pl.ds(lane, LANE)] = value.astype(BF16)
+        return carry
+
+    base = 0
+    for k, count in enumerate(blocks):
+
+        def bucket(base=base, count=count, k=k):
             def one(g, carry):
                 for i in range(group):
-                    top = pl.multiple_of((base + i * count) * ROWS, ROWS)
-                    rows = pl.ds(top, count * ROWS)
+                    rows = pl.ds((base + i * count) * ROWS, count * ROWS)
                     y = jnp.dot(x_ref[rows, :], t_ref[g, i], preferred_element_type=F32)
                     re = im = None
                     for b in range(count):
@@ -273,65 +264,126 @@
                         add_im = w_cos * y_im - w_sin * y_re
                         re = add_re if re is None else re + add_re
                         im = add_im if im is None else im + add_im
-                    j = stage * group + i
                     for a, part in enumerate((re, im)):
                         part = part.astype(BF16).astype(F32)
                         north, south = part[0:8], part[8:16]
                         for s, total in enumerate((north + south, north - south)):
-                            start = (s * 2 * lf + a * lf) * pairs + j
-                            f_ref[g, pl.ds(start, lf, stride=pairs), :] = total[0:lf]
+                            start = (s * 2 * lf + a * lf) * (group + 1) + i
+                            f_ref[g, pl.ds(start, lf, stride=group + 1), :] = total[0:lf]
                 return carry
 
             lax.fori_loop(0, many, one, 0)
-
-        pl.when((stage >= begin) & (stage < end))(bucket)
-        first += count * group * (end - begin)
-        begin = end
-
-    piece = 16 if pairs % 16 == 0 else pairs
-
-    def pack():
-        def one(step, carry):
-            g, start = step // (pairs // piece), step % (pairs // piece) * piece
-            for cg in range(cgs):
-                items = []
-                for p in range(cg * waves, (cg + 1) * waves):
-                    if p < len(order):
-                        kind, row = order[p]
-                        top = pl.multiple_of((kind * 2 * lf + row) * pairs + start, 8)
-                        items.append(f_ref[g, pl.ds(top, piece), :])
-                    else:
-                        items.append(jnp.zeros((piece, LANE), F32))
-                lane = pl.multiple_of((g * cgs + cg) * LANE, LANE)
-                for d, value in enumerate(swap_blocks(items, LANE // waves)):
-                    top = pl.multiple_of(d * pairs + start, piece)
-                    o_ref[pl.ds(top, piece), pl.ds(lane, LANE)] = value.astype(BF16)
-            return carry
-
-        lax.fori_loop(0, many * (pairs // piece), one, 0, unroll=pairs // piece)
-
-    pl.when(stage == len(blocks) - 1)(pack)
+            lax.fori_loop(0, many, functools.partial(pack, k * group), 0)
+
+        pl.when(stage == k)(bucket)
+        base += count * group
+
+def rows_kernel(blocks, lf, waves, pairs, k_ref, t_ref, w_ref, o_ref, f_ref, x_ref, sems):
+    step = pl.program_id(0)
+    group = pairs // len(blocks)
+    copies = []
+    base = 0
+    for k, count in enumerate(blocks):
+        rows = pl.ds(base * ROWS, count * group * ROWS)
+        copies.append(pltpu.make_async_copy(k_ref.at[rows], x_ref.at[rows], sems.at[k]))
+        base += count * group
+
+    def begin():
+        for copy in copies:
+            copy.start()
+
+    pl.when(step == 0)(begin)
+    for k, copy in enumerate(copies):
+        pl.when(step == k)(copy.wait)
+    rows_stage(blocks, lf, waves, pairs, step, x_ref, t_ref, w_ref, o_ref, f_ref)
+
+
+def first_kernel(
+    blocks, lf, waves, pairs, slot_ref, room_ref, a_ref, ahead_ref, t_ref, w_ref, o_ref, k_ref,
+    f_ref, s_ref, x_ref, sem
+):
+    del ahead_ref
+    step = pl.program_id(0)
+    group = pairs // len(blocks)
+    keep = pltpu.make_async_copy(x_ref, k_ref, sem)
+
+    def begin():
+        place_tiles(blocks, group, slot_ref, room_ref, a_ref, x_ref, s_ref)
+        keep.start()
+
+    pl.when(step == 0)(begin)
+    rows_stage(blocks, lf, waves, pairs, step - 1, x_ref, t_ref, w_ref, o_ref, f_ref)
+    pl.when(step == len(blocks))(keep.wait)
+
+
+def table_specs(table, blocks, lag):
+    ng, pairs, rows, lanes = table.shape
+    at = lambda k, *_: (0, jnp.maximum(k - lag, 0), 0, 0)
+    group = pairs // len(blocks)
+    return [
+        pl.BlockSpec((ng, group, rows, lanes), at),
+        pl.BlockSpec((ng, group, 2 * ROWS, LANE), at),
+    ]
+
+
+def rows_cost(blocks, table, twist):
+    ng, pairs, rows, lanes = table.shape
+    taps = sum(blocks) * (pairs // len(blocks)) * ROWS * rows
+    return cost(ng * 2 * taps * lanes, 2 * taps + 2 * table.size + 4 * twist.size)
+
+
+def first_rows(arrived, slots, room, ahead, table, twist, blocks, lf, waves):
+    sources, share, fields, cap, width = arrived.shape
+    ng, pairs = table.shape[:2]
+    cgs = -(-4 * lf // waves)
+    return pl.pallas_call(
+        functools.partial(first_kernel, blocks, lf, waves, pairs),
+        grid_spec=pltpu.PrefetchScalarGridSpec(
+            num_scalar_prefetch=2,
+            grid=(len(blocks) + 1,),
+            in_specs=[
+                pl.BlockSpec(memory_space=pltpu.VMEM),
+                pl.BlockSpec(memory_space=pl.ANY),
+            ]
+            + table_specs(table, blocks, 1),
+            out_specs=[
+                pl.BlockSpec((waves * pairs, ng * cgs * LANE), lambda k, *_: (0, 0)),
+                pl.BlockSpec(memory_space=pl.ANY),
+            ],
+            scratch_shapes=[
+                pltpu.VMEM((ng, 4 * lf * (pairs // len(blocks) + 1), LANE), F32),
+                pltpu.VMEM((TILE // LANE, sources * cap * SPAN, LANE), F32),
+                pltpu.VMEM((slots.shape[0] * ROWS, TILE), BF16),
+                pltpu.SemaphoreType.DMA,
+            ],
+        ),
+        out_shape=[
+            pltpu.HBM((waves * pairs, ng * cgs * LANE), BF16),
+            pltpu.HBM((slots.shape[0] * ROWS, TILE), BF16),
+        ],
+        compiler_params=params(57),
+        cost_estimate=rows_cost(blocks, table, twist),
+        name="place_and_rows",
+    )(slots, room, arrived, ahead, table, twist)
 
 
 def rows_to_waves(tiles, table, twist, blocks, lf, waves):
     ng, pairs = table.shape[:2]
-    group = group_of(pairs)
     cgs = -(-4 * lf // waves)
     return pl.pallas_call(
         functools.partial(rows_kernel, blocks, lf, waves, pairs),
         grid=(len(blocks),),
-        in_specs=[
-            pl.BlockSpec(tiles.shape, lambda k: (0, 0)),
-            pl.BlockSpec((ng, group, TILE, 2 * LANE), lambda k: (0, k, 0, 0)),
-            pl.BlockSpec((ng, group, 2 * ROWS, LANE), lambda k: (0, k, 0, 0)),
+        in_specs=[pl.BlockSpec(memory_space=pl.ANY)]
+        + table_specs(table, blocks, 0),
+        out_specs=pl.BlockSpec((waves * pairs, ng * cgs * LANE), lambda k: (0, 0)),
+        out_shape=pltpu.HBM((waves * pairs, ng * cgs * LANE), BF16),
+        scratch_shapes=[
+            pltpu.VMEM((ng, 4 * lf * (pairs // len(blocks) + 1), LANE), F32),
+            pltpu.VMEM(tiles.shape, BF16),
+            pltpu.SemaphoreType.DMA((len(blocks),)),
         ],
-        out_specs=pl.BlockSpec((waves * pairs, ng * cgs * LANE), lambda k: (0, 0)),
-        out_shape=jax.ShapeDtypeStruct((waves * pairs, ng * cgs * LANE), BF16),
-        scratch_shapes=[pltpu.VMEM((ng, 4 * lf * pairs, LANE), F32)],
-        compiler_params=params(56),
-        cost_estimate=cost(
-            ng * 2 * tiles.size * 2 * LANE, 2 * tiles.size + 2 * table.size + 4 * twist.size
-        ),
+        compiler_params=params(60),
+        cost_estimate=rows_cost(blocks, table, twist),
         name="rows_to_waves",
     )(tiles, table, twist)
 
@@ -339,6 +391,7 @@
 def legendre_kernel(g0, per_group, waves, lf, total, own_ref, r_ref, p_ref, l_ref, *rest):
     s_ref, o_ref, d_ref, b_ref = rest[-4:]
     width = LANE // waves
+    span = width + 1
     group, stage = pl.program_id(0), pl.program_id(1)
     many = l_ref.shape[0]
     order = row_order(lf)
@@ -351,8 +404,11 @@
         value = lax.dot_general(
             r_ref[...], p_ref[...], (((0,), (0,)), ((), ())), preferred_element_type=F32
         )
-        for t in range(lanes):
-            d_ref[t] = value[:, t * LANE : (t + 1) * LANE]
+        for p in range(rows // width):
+            for t in range(lanes):
+                d_ref[t, p * span : p * span + width, :] = value[
+                    p * width : (p + 1) * width, t * LANE : (t + 1) * LANE
+                ]
         if rows > len(order) * width:
             b_ref[...] = jnp.zeros_like(b_ref)
 
@@ -365,9 +421,7 @@
         q = own_ref[(g0 + group) * per_group + local]
 
         def where_rows(w, tile, local=local):
-            p = tile * 8
-            start = p // waves * LANE + p % waves * width + 2 * local + w
-            return pl.ds(start, 8, stride=width)
+            return pl.ds(tile * 8 * span + 2 * local + w, 8, stride=span)
 
         picked = []
         for w in range(2):
@@ -407,7 +461,11 @@
                     b_ref[t, cut, :] = rebuilt[row : row + 8, t * LANE : (t + 1) * LANE]
 
     def end():
-        value = jnp.concatenate([b_ref[t].astype(BF16) for t in range(lanes)], axis=1)
+        lines = []
+        for p in range(rows // width):
+            cut = pl.ds(p * span, width)
+            lines.append(jnp.concatenate([b_ref[t, cut, :] for t in range(lanes)], axis=1))
+        value = jnp.concatenate(lines, axis=0).astype(BF16)
         o_ref[...] = lax.dot_general(
             p_ref[...], value, (((1,), (1,)), ((), ())), preferred_element_type=F32
         ).astype(BF16)
@@ -446,16 +504,16 @@
                 pl.BlockSpec((pair_total, rows), lambda g, k, *_: (0, g)),
             ],
             scratch_shapes=[
-                pltpu.VMEM((pair_total // LANE, rows, LANE), F32),
-                pltpu.VMEM((pair_total // LANE, rows, LANE), F32),
+                pltpu.VMEM((pair_total // LANE, cgs * (LANE + waves), LANE), F32),
+                pltpu.VMEM((pair_total // LANE, cgs * (LANE + waves), LANE), F32),
             ],
         ),
         out_shape=[
             jax.ShapeDtypeStruct((sets, 2 * lf, coefs), F32),
-            jax.ShapeDtypeStruct((pair_total, ng * rows), BF16),
+            pltpu.HBM((pair_total, ng * rows), BF16),
         ],
         input_output_aliases=aliases,
-        compiler_params=params(48),
+        compiler_params=params(60),
         cost_estimate=cost(
             ng * per_group * 4 * 48 * coefs * pair_total, ng * per_group * 2 * coefs * pair_total
         ),
@@ -540,8 +598,7 @@
     blocks = []
     for k in range(stages):
         largest = waves * (k * group + group - 1) + waves - 1
-        least = min(BLK, -(-(4 * largest + 20) // TILE))
-        blocks.append(min(x for x in STEPS if x >= least))
+        blocks.append(min(BLK, -(-(4 * largest + 20) // TILE)))
     pair_at = [k * group + i for k in range(stages) for i in range(group) for _ in range(blocks[k])]
     block_at = [b for k in range(stages) for i in range(group) for b in range(blocks[k])]
     pair_at = jnp.asarray(pair_at, jnp.int32)
@@ -555,8 +612,6 @@
     found = jnp.where(own[None, :] == wanted[:, None], slot_ids[None, :], 0)
     slot_of = jnp.max(found, axis=1)
 
-    tiles = gather_tiles(arrived, slot_of, room, legendre)
-
     places = (pair_order[:, None] == jnp.arange(pair_total, dtype=jnp.int32)[None, :]).astype(BF16)
     own_sets = lax.dynamic_slice_in_dim(m_order, me * sets, sets)
     lane = jnp.arange(waves_total, dtype=jnp.int32)
@@ -566,9 +621,11 @@
 
     received = []
     for c in range(len(chunks)):
-        sent = rows_to_waves(
-            tiles, tables[2 * c], tables[2 * c + 1], tuple(blocks), lf, waves
-        )
+        pieces = tables[2 * c], tables[2 * c + 1], tuple(blocks), lf, waves
+        if c == 0:
+            sent, tiles = first_rows(arrived, slot_of, room, legendre, *pieces)
+        else:
+            sent = rows_to_waves(tiles, *pieces)
         received.append(lax.all_to_all(sent, "wave", 0, 0, tiled=True))
     spectral = None
     returned = []

time: 222 us -> 211 us (0.950)
  Pallas kernels: 129 us -> 121 us
  local copies, waits for them, and re-layouts: 40.9 us -> 37.6 us
    pallas_call x2 -> x1, Pallas kernels: 38 us -> 19.3 us  [rows_to_waves(): pl.pallas_call(functools.partial(rows_kernel, blocks, lf, waves, pairs),...]
    pallas_call x1, Pallas kernels: 7.81 us -> 18.7 us  [first_rows(): pl.pallas_call(functools.partial(first_kernel, blocks, lf, waves, pairs),...]
    unnamed x29 -> x21, local copies, waits for them, and re-layouts: 34.9 us -> 30.1 us
  transfers between devices with their start and end apart: 5 -> 5, of which waited for: 3 -> 3; matrix products, arithmetic and copies ran while one was open for 15% -> 17% of each run, Pallas kernels for 41% -> 42%
where the time goes in v2:
time: 211 us
  Pallas kernels  121 us (57%)
  local copies, waits for them, and re-layouts  37.6 us (18%)
  waiting for transfers between devices  24.9 us (12%)
  starting transfers between devices  23.2 us (11%)
  other arithmetic  2.93 us (1%)
    pallas_call x1, Pallas kernels, phase_tables(): pl.pallas_call(functools.partial(table_kernel, chunks), grid_spec=pltpu.P...  35 us
    pallas_call x2, Pallas kernels, legendre_both(): pl.pallas_call(functools.partial(legendre_kernel, g0, per_group, waves, l...  34.9 us
    unnamed x21, local copies, waits for them, and re-layouts  30.1 us
    pallas_call x1, Pallas kernels, rows_to_waves(): pl.pallas_call(functools.partial(rows_kernel, blocks, lf, waves, pairs),...  19.3 us
    pallas_call x1, Pallas kernels, first_rows(): pl.pallas_call(functools.partial(first_kernel, blocks, lf, waves, pairs),...  18.7 us
    all_to_all x2, waiting for transfers between devices, body(): returned.append(lax.all_to_all(back, 'wave', 0, 0, tiled=True))  15.5 us
    all_to_all x2, starting transfers between devices, body(): received.append(lax.all_to_all(sent, 'wave', 0, 0, tiled=True))  8.26 us
    all_to_all x2, starting transfers between devices, body(): returned.append(lax.all_to_all(back, 'wave', 0, 0, tiled=True))  7.67 us
  transfers between devices with their start and end apart: 5, of which 3 were waited for; matrix products, arithmetic and copies ran while one was open for 17% of the time, Pallas kernels for 42%

profile of v2, /device:TPU:0, one launch (start us, length us, event | category | flops | bytes accessed | tf_op | source)
XLA Modules:
  0.0 210.7 jit_solution(16958889496050948349)
XLA Ops:
  0.6 7.6 %diffuse.1 = bf16[8,4,2,3,16,512]{5,4,3,2,1,0:T(8,128)(2,1)} custom-call(f32[8,3,8,16,512]{4,3,2,1,0:T(8,128)} %bitcast.16, bf16[7,8,16,512]{3,2,1,0:T(8,128)(2,1)} %bitcast.24), custom_call_target="tpu_custom_call" | custom-call | flops 62914560 | bytes 10354688 | tf_op jit(solution)/shard_map/diffuse/pallas_call | solution.py:100
  8.2 0.0 copy-start.4
  8.2 0.0 copy-start.3
  8.2 7.3 %all-to-all-start = ((bf16[32,2,3,16,512]{4,3,2,1,0:T(8,128)(2,1)}), bf16[32,2,3,16,512]{4,3,2,1,0:T(8,128)(2,1)S(1)}, u32[]{:S(2)}, u32[]{:S(2)}) async-start(bf16[32,2,3,16,512]{4,3,2,1,0:T(8,128)(2,1)} %bitcast.15), calls=%async_computation | async-start | bytes 6291456 | tf_op jit(solution)/shard_map/all_to_all | solution.py:587
  15.5 0.0 copy-done.4
  15.6 0.1 copy.23
  15.8 0.1 convert_element_type.20
  15.9 0.1 convert_element_type.22.m_ref
  16.0 0.0 copy-done.3
  16.0 0.1 reshape.133
  16.1 0.1 dynamic-slice_reduce_fusion
  16.1 0.1 eq.45
  16.2 0.0 copy-start.5
  16.2 0.0 copy-start.8
  16.2 23.1 %copy.25.ahead_ref.l_ref = bf16[40,641,640]{2,1,0:T(8,128)(2,1)} copy(bf16[40,641,640]{2,0,1:T(8,128)(2,1)} %param.13) | data formatting | bytes 65638400 | tf_op args[5]
  39.3 0.0 copy-done.5
  39.3 0.1 fusion.29
  39.4 0.0 copy-done.8
  39.4 0.0 copy-start.6
  39.4 0.0 copy-start.7
  39.4 3.8 %gather_fusion = s32[560]{0:T(1024)S(1)} fusion(s32[80]{0:T(128)S(1)} %get-tuple-element.29, s32[1024]{0:T(1024)S(1)} %pad_clamp_fusion), kind=kCustom, calls=%fused_computation | custom fusion | bytes 6720 | tf_op jit(solution)/shard_map/jit(_take)/gather | solution.py:606
  43.3 35.0 %tables.1 = (bf16[2,80,256,256]{3,2,1,0:T(8,128)(2,1)}, f32[2,80,32,128]{3,2,1,0:T(8,128)}, bf16[3,80,256,256]{3,2,1,0:T(8,128)(2,1)}, f32[3,80,32,128]{3,2,1,0:T(8,128)}) custom-call(f32[80]{0:T(128)S(1)} %add_convert_fusion.1.count_ref, f32[80]{0:T(128)S(1)} %broadcast_divide_fusion.inverse_ref, f32[80]{0:T(128)S(1)} %get-tuple-element.28.scale_ref, ...), custom_call_target="tpu_custom_call" | custom-call | flops 262144000 | bytes 52428800 | tf_op jit(solution)/shard_map/tables/pallas_call | solution.py:177
  78.3 0.0 copy-done.6
  78.3 0.0 copy-done.7
  78.3 0.6 add_add_fusion
  78.9 0.9 select_reduce_fusion.slot_ref
  79.8 5.9 %all-to-all-done.a_ref = bf16[32,2,3,16,512]{4,3,2,1,0:T(8,128)(2,1)S(1)} async-done(((bf16[32,2,3,16,512]{4,3,2,1,0:T(8,128)(2,1)}), bf16[32,2,3,16,512]{4,3,2,1,0:T(8,128)(2,1)S(1)}, u32[]{:S(2)}, u32[]{:S(2)}) %all-to-all-start) | async-done | bytes 3145760 | tf_op jit(solution)/shard_map/all_to_all | solution.py:587
  85.7 0.0 copy-start
  85.7 1.8 copy-done
  87.5 18.7 %place_and_rows.1 = (bf16[640,768]{1,0:T(8,128)(2,1)}, bf16[8960,256]{1,0:T(8,128)(2,1)}) custom-call(s32[560]{0:T(1024)} %select_reduce_fusion.slot_ref, s32[560]{0:T(1024)} %get-tuple-element.30.room_ref, bf16[32,2,3,16,512]{4,3,2,1,0:T(8,128)(2,1)} %copy-done, bf16[40,641,640]{2,1,0:T(8,128)(2,1)} %copy.25.ahead_ref.l_ref, ...), custom_call_target="tpu_custom_call" | custom-call | flops 2348810240 | bytes 28180480 | tf_op jit(solution)/shard_map/place_and_rows/pallas_call | solution.py:339
  106.2 4.1 %all-to-all-start.2 = ((bf16[8,80,768]{2,1,0:T(8,128)(2,1)}), bf16[8,80,768]{2,1,0:T(8,128)(2,1)S(1)}, u32[]{:S(2)}, u32[]{:S(2)}) async-start(bf16[8,80,768]{2,1,0:T(8,128)(2,1)} %bitcast.23), calls=%async_computation.2 | async-start | bytes 1966080 | tf_op jit(solution)/shard_map/all_to_all | solution.py:629
  110.3 19.3 %rows_to_waves.1 = bf16[640,1152]{1,0:T(8,128)(2,1)} custom-call(bf16[8960,256]{1,0:T(8,128)(2,1)} %get-tuple-element.14.k_ref, bf16[3,80,256,256]{3,2,1,0:T(8,128)(2,1)} %get-tuple-element.15.t_ref, f32[3,80,32,128]{3,2,1,0:T(8,128)} %get-tuple-element.16.w_ref), custom_call_target="tpu_custom_call" | custom-call | flops 3523215360 | bytes 39976960 | tf_op jit(solution)/shard_map/rows_to_waves/pallas_call | solution.py:373
  129.6 0.0 all-to-all-done.2
  129.6 0.0 copy-start.2
  129.6 4.2 %all-to-all-start.1 = ((bf16[8,80,1152]{2,1,0:T(8,128)(2,1)}), bf16[8,80,1152]{2,1,0:T(8,128)(2,1)S(1)}, u32[]{:S(2)}, u32[]{:S(2)}) async-start(bf16[8,80,1152]{2,1,0:T(8,128)(2,1)} %bitcast.19), calls=%async_computation.1 | async-start | bytes 2949120 | tf_op jit(solution)/shard_map/all_to_all | solution.py:629
  133.8 0.7 dynamic_slice.10.own_ref
  134.5 1.1 fusion.p_ref
  135.5 0.0 copy-done.2
  135.5 14.7 %legendre.2 = (f32[40,12,641]{2,1,0:T(8,128)}, bf16[640,768]{1,0:T(8,128)(2,1)}) custom-call(s32[40]{0:T(128)} %dynamic_slice.10.own_ref, bf16[640,768]{1,0:T(8,128)(2,1)} %bitcast.20, bf16[640,640]{1,0:T(8,128)(2,1)} %fusion.p_ref, bf16[40,641,640]{2,1,0:T(8,128)(2,1)} %copy.25.ahead_ref.l_ref), custom_call_target="tpu_custom_call" | custom-call | flops 1260257280 | bytes 13127680 | tf_op jit(solution)/shard_map/legendre/pallas_call | solution.py:496
  150.2 3.5 %all-to-all-done.1 = bf16[8,80,1152]{2,1,0:T(8,128)(2,1)S(1)} async-done(((bf16[8,80,1152]{2,1,0:T(8,128)(2,1)}), bf16[8,80,1152]{2,1,0:T(8,128)(2,1)S(1)}, u32[]{:S(2)}, u32[]{:S(2)}) %all-to-all-start.1) | async-done | bytes 1474592 | tf_op jit(solution)/shard_map/all_to_all | solution.py:629
  153.8 0.0 copy-start.1
  153.8 3.6 %all-to-all-start.3 = ((bf16[8,80,768]{2,1,0:T(8,128)(2,1)}), bf16[8,80,768]{2,1,0:T(8,128)(2,1)S(1)}, u32[]{:S(2)}, u32[]{:S(2)}) async-start(bf16[8,80,768]{2,1,0:T(8,128)(2,1)} %bitcast.22), calls=%async_computation.3 | async-start | bytes 1966080 | tf_op jit(solution)/shard_map/all_to_all | solution.py:638
  157.3 0.0 copy-done.1
  157.3 20.2 %legendre.3 = (f32[40,12,641]{2,1,0:T(8,128)}, bf16[640,1152]{1,0:T(8,128)(2,1)}) custom-call(s32[40]{0:T(128)} %dynamic_slice.10.own_ref, bf16[640,1152]{1,0:T(8,128)(2,1)} %bitcast.18, bf16[640,640]{1,0:T(8,128)(2,1)} %fusion.p_ref, bf16[40,641,640]{2,1,0:T(8,128)(2,1)} %copy.25.ahead_ref.l_ref, ...), custom_call_target="tpu_custom_call", output_to_operand_aliasing={{0}: (4, {})} | custom-call | flops 1890385920 | bytes 19691520 | tf_op jit(solution)/shard_map/legendre/pallas_call | solution.py:496
  177.5 0.0 all-to-all-done.3.refs_0_
  177.6 4.1 %all-to-all-start.4 = ((bf16[8,80,1152]{2,1,0:T(8,128)(2,1)}), bf16[8,80,1152]{2,1,0:T(8,128)(2,1)S(1)}, u32[]{:S(2)}, u32[]{:S(2)}) async-start(bf16[8,80,1152]{2,1,0:T(8,128)(2,1)} %bitcast.21), calls=%async_computation.4 | async-start | bytes 2949120 | tf_op jit(solution)/shard_map/all_to_all | solution.py:638
  181.7 0.2 fusion.1.refs_2_
  181.9 2.4 %copy.28 = f32[40,12,641]{2,0,1:T(8,128)S(1)} copy(f32[40,12,641]{2,1,0:T(8,128)} %get-tuple-element.19) | data formatting | bytes 2461440 | tf_op jit(solution)/shard_map/legendre/pallas_call | solution.py:496
  184.3 1.9 copy.29
  186.2 15.5 %all-to-all-done.4.refs_1_ = bf16[8,80,1152]{2,1,0:T(8,128)(2,1)S(1)} async-done(((bf16[8,80,1152]{2,1,0:T(8,128)(2,1)}), bf16[8,80,1152]{2,1,0:T(8,128)(2,1)S(1)}, u32[]{:S(2)}, u32[]{:S(2)}) %all-to-all-start.4) | async-done | bytes 1474592 | tf_op jit(solution)/shard_map/all_to_all | solution.py:638
  201.6 5.7 %unpack.1 = bf16[24,80,640]{2,1,0:T(8,128)(2,1)S(1)} custom-call(bf16[8,80,768]{2,1,0:T(8,128)(2,1)S(1)} %all-to-all-done.3.refs_0_, bf16[8,80,1152]{2,1,0:T(8,128)(2,1)S(1)} %all-to-all-done.4.refs_1_, bf16[640,640]{1,0:T(8,128)(2,1)S(1)} %fusion.1.refs_2_), custom_call_target="tpu_custom_call" | custom-call | flops 1572864000 | bytes 4915200 | tf_op jit(solution)/shard_map/unpack/pallas_call | solution.py:553
  207.3 3.3 %copy.30 = bf16[80,2,2,3,2,640]{5,4,3,2,1,0:T(2,128)(2,1)} copy(bf16[80,2,2,3,2,640]{5,0,4,3,2,1:T(8,128)(2,1)S(1)} %bitcast.14) | data formatting | bytes 4915200
  (9 shorter events, 0.1 us)
Async XLA Ops:
  8.2 7.3 %copy-start.4 = (s32[320]{0:T(512)S(1)}, s32[320]{0:T(512)}, u32[]{:S(2)}) copy-start(s32[320]{0:T(512)} %param.12) | copy-start | bytes 3844
  8.2 7.7 %copy-start.3 = (s32[4096]{0:T(1024)S(1)}, s32[4096]{0:T(1024)}, u32[]{:S(2)}) copy-start(s32[4096]{0:T(1024)} %param.10) | copy-start | bytes 49156
  8.2 77.5 %all-to-all-start = ((bf16[32,2,3,16,512]{4,3,2,1,0:T(8,128)(2,1)}), bf16[32,2,3,16,512]{4,3,2,1,0:T(8,128)(2,1)S(1)}, u32[]{:S(2)}, u32[]{:S(2)}) async-start(bf16[32,2,3,16,512]{4,3,2,1,0:T(8,128)(2,1)} %bitcast.15), calls=%async_computation | async-start | bytes 6291456 | tf_op jit(solution)/shard_map/all_to_all | solution.py:587
  16.2 23.1 %copy-start.5 = (s32[640]{0:T(1024)S(1)}, s32[640]{0:T(1024)}, u32[]{:S(2)}) copy-start(s32[640]{0:T(1024)} %param.11) | copy-start | bytes 7684
  16.2 23.2 %copy-start.8 = (s32[560]{0:T(1024)S(1)}, s32[560]{0:T(1024)}, u32[]{:S(2)}) copy-start(s32[560]{0:T(1024)} %constant.137) | copy-start | bytes 6724
  39.4 38.9 %copy-start.6 = (s32[560]{0:T(1024)S(1)}, s32[560]{0:T(1024)}, u32[]{:S(2)}) copy-start(s32[560]{0:T(1024)} %constant.126.clone) | copy-start | bytes 6724
  39.4 38.9 %copy-start.7 = (s32[560]{0:T(1024)S(1)}, s32[560]{0:T(1024)}, u32[]{:S(2)}) copy-start(s32[560]{0:T(1024)} %constant.136) | copy-start | bytes 6724
  85.7 1.8 copy-start
  106.2 23.4 %all-to-all-start.2 = ((bf16[8,80,768]{2,1,0:T(8,128)(2,1)}), bf16[8,80,768]{2,1,0:T(8,128)(2,1)S(1)}, u32[]{:S(2)}, u32[]{:S(2)}) async-start(bf16[8,80,768]{2,1,0:T(8,128)(2,1)} %bitcast.23), calls=%async_computation.2 | async-start | bytes 1966080 | tf_op jit(solution)/shard_map/all_to_all | solution.py:629
  129.6 6.0 %copy-start.2 = (bf16[8,80,768]{2,1,0:T(8,128)(2,1)}, bf16[8,80,768]{2,1,0:T(8,128)(2,1)S(1)}, u32[]{:S(2)}) copy-start(bf16[8,80,768]{2,1,0:T(8,128)(2,1)S(1)} %all-to-all-done.2) | copy-start | bytes 2949124
  129.6 24.2 %all-to-all-start.1 = ((bf16[8,80,1152]{2,1,0:T(8,128)(2,1)}), bf16[8,80,1152]{2,1,0:T(8,128)(2,1)S(1)}, u32[]{:S(2)}, u32[]{:S(2)}) async-start(bf16[8,80,1152]{2,1,0:T(8,128)(2,1)} %bitcast.19), calls=%async_computation.1 | async-start | bytes 2949120 | tf_op jit(solution)/shard_map/all_to_all | solution.py:629
  153.8 3.6 %copy-start.1 = (bf16[8,80,1152]{2,1,0:T(8,128)(2,1)}, bf16[8,80,1152]{2,1,0:T(8,128)(2,1)S(1)}, u32[]{:S(2)}) copy-start(bf16[8,80,1152]{2,1,0:T(8,128)(2,1)S(1)} %all-to-all-done.1) | copy-start | bytes 4423684
  153.8 23.8 %all-to-all-start.3 = ((bf16[8,80,768]{2,1,0:T(8,128)(2,1)}), bf16[8,80,768]{2,1,0:T(8,128)(2,1)S(1)}, u32[]{:S(2)}, u32[]{:S(2)}) async-start(bf16[8,80,768]{2,1,0:T(8,128)(2,1)} %bitcast.22), calls=%async_computation.3 | async-start | bytes 1966080 | tf_op jit(solution)/shard_map/all_to_all | solution.py:638
  177.6 24.1 %all-to-all-start.4 = ((bf16[8,80,1152]{2,1,0:T(8,128)(2,1)}), bf16[8,80,1152]{2,1,0:T(8,128)(2,1)S(1)}, u32[]{:S(2)}, u32[]{:S(2)}) async-start(bf16[8,80,1152]{2,1,0:T(8,128)(2,1)} %bitcast.21), calls=%async_computation.4 | async-start | bytes 2949120 | tf_op jit(solution)/shard_map/all_to_all | solution.py:638

commit v3 on v2

--- a/solution.py
+++ b/solution.py
@@ -16,6 +16,7 @@
 BF16 = jnp.bfloat16
 MIB = 1024 * 1024
 CHUNKS = (2, 3)
+OWNERS = 4
 
 
 def group_of(pairs):
@@ -64,9 +65,9 @@
 def diffuse_kernel(share, x_ref, a_ref, o_ref):
     levels, fields = x_ref.shape[0], x_ref.shape[1]
     width = x_ref.shape[-1]
-    for start in range(0, width, LANE):
+    for w, start in [(w, start) for w in range(x_ref.shape[2]) for start in range(0, width, LANE)]:
         cut = pl.ds(start, LANE)
-        coef = [a_ref[k, 0, :, cut].astype(F32) for k in range(levels - 1)]
+        coef = [a_ref[k, w, :, cut].astype(F32) for k in range(levels - 1)]
         ratios = []
         partials = [[] for _ in range(fields)]
         for k in range(levels):
@@ -80,7 +81,7 @@
             if k < levels - 1:
                 ratios.append(coef[k] * inverse)
             for f in range(fields):
-                value = x_ref[k, f, 0, :, cut]
+                value = x_ref[k, f, w, :, cut]
                 if k:
                     value = value + coef[k - 1] * partials[f][k - 1]
                 partials[f].append(value * inverse)
@@ -88,7 +89,7 @@
             solved = None
             for k in range(levels - 1, -1, -1):
                 solved = partials[f][k] if solved is None else partials[f][k] + ratios[k] * solved
-                o_ref[0, k // share, k % share, f, :, cut] = solved.astype(BF16)
+                o_ref[w, k // share, k % share, f, :, cut] = solved.astype(BF16)
 
 
 def diffuse(grid_fields, diffusivity, waves, groups):
@@ -99,12 +100,12 @@
     a = diffusivity.reshape(levels - 1, waves, cap, width)
     return pl.pallas_call(
         functools.partial(diffuse_kernel, share),
-        grid=(waves,),
+        grid=(waves // OWNERS,),
         in_specs=[
-            pl.BlockSpec((levels, fields, 1, cap, width), lambda w: (0, 0, w, 0, 0)),
-            pl.BlockSpec((levels - 1, 1, cap, width), lambda w: (0, w, 0, 0)),
+            pl.BlockSpec((levels, fields, OWNERS, cap, width), lambda w: (0, 0, w, 0, 0)),
+            pl.BlockSpec((levels - 1, OWNERS, cap, width), lambda w: (0, w, 0, 0)),
         ],
-        out_specs=pl.BlockSpec((1, groups, share, fields, cap, width), lambda w: (w, 0, 0, 0, 0, 0)),
+        out_specs=pl.BlockSpec((OWNERS, groups, share, fields, cap, width), lambda w: (w, 0, 0, 0, 0, 0)),
         out_shape=jax.ShapeDtypeStruct((waves, groups, share, fields, cap, width), BF16),
         compiler_params=params(60),
         cost_estimate=cost(40 * x.size, 6 * x.size + 2 * a.size),
@@ -361,7 +362,7 @@
             pltpu.HBM((waves * pairs, ng * cgs * LANE), BF16),
             pltpu.HBM((slots.shape[0] * ROWS, TILE), BF16),
         ],
-        compiler_params=params(57),
+        compiler_params=params(48),
         cost_estimate=rows_cost(blocks, table, twist),
         name="place_and_rows",
     )(slots, room, arrived, ahead, table, twist)

time: 211 us -> 207 us (0.981)
  Pallas kernels: 121 us -> 117 us
    pallas_call x1, Pallas kernels: 7.6 us -> 5.05 us  [diffuse(): pl.pallas_call(functools.partial(diffuse_kernel, share), grid=(waves // O...]
  transfers between devices with their start and end apart: 5 -> 5, of which waited for: 3 -> 3; matrix products, arithmetic and copies ran while one was open for 17% -> 17% of each run, Pallas kernels for 42% -> 43%
where the time goes in v3:
time: 207 us
  Pallas kernels  117 us (57%)
  local copies, waits for them, and re-layouts  37.5 us (18%)
  waiting for transfers between devices  25.9 us (13%)
  starting transfers between devices  23.2 us (11%)
    pallas_call x1, Pallas kernels, phase_tables(): pl.pallas_call(functools.partial(table_kernel, chunks), grid_spec=pltpu.P...  35.1 us
    pallas_call x2, Pallas kernels, legendre_both(): pl.pallas_call(functools.partial(legendre_kernel, g0, per_group, waves, l...  34.9 us
    unnamed x21, local copies, waits for them, and re-layouts  30.1 us
    pallas_call x1, Pallas kernels, rows_to_waves(): pl.pallas_call(functools.partial(rows_kernel, blocks, lf, waves, pairs),...  19.3 us
    pallas_call x1, Pallas kernels, first_rows(): pl.pallas_call(functools.partial(first_kernel, blocks, lf, waves, pairs),...  17.3 us
    all_to_all x2, waiting for transfers between devices, body(): returned.append(lax.all_to_all(back, 'wave', 0, 0, tiled=True))  15.5 us
    all_to_all x2, starting transfers between devices, body(): received.append(lax.all_to_all(sent, 'wave', 0, 0, tiled=True))  8.25 us
    all_to_all x2, starting transfers between devices, body(): returned.append(lax.all_to_all(back, 'wave', 0, 0, tiled=True))  7.67 us
  transfers between devices with their start and end apart: 5, of which 3 were waited for; matrix products, arithmetic and copies ran while one was open for 17% of the time, Pallas kernels for 43%

profile of v3, /device:TPU:0, one launch (start us, length us, event | category | flops | bytes accessed | tf_op | source)
XLA Modules:
  0.0 206.6 jit_solution(14174691087099489898)
XLA Ops:
  0.6 5.0 %diffuse.1 = bf16[8,4,2,3,16,512]{5,4,3,2,1,0:T(8,128)(2,1)} custom-call(f32[8,3,8,16,512]{4,3,2,1,0:T(8,128)} %bitcast.16, bf16[7,8,16,512]{3,2,1,0:T(8,128)(2,1)} %bitcast.24), custom_call_target="tpu_custom_call" | custom-call | flops 62914560 | bytes 10354688 | tf_op jit(solution)/shard_map/diffuse/pallas_call | solution.py:101
  5.7 0.0 copy-start.4
  5.7 0.0 copy-start.3
  5.7 7.3 %all-to-all-start = ((bf16[32,2,3,16,512]{4,3,2,1,0:T(8,128)(2,1)}), bf16[32,2,3,16,512]{4,3,2,1,0:T(8,128)(2,1)S(1)}, u32[]{:S(2)}, u32[]{:S(2)}) async-start(bf16[32,2,3,16,512]{4,3,2,1,0:T(8,128)(2,1)} %bitcast.15), calls=%async_computation | async-start | bytes 6291456 | tf_op jit(solution)/shard_map/all_to_all | solution.py:588
  13.0 0.0 copy-done.4
  13.1 0.1 copy.23
  13.2 0.1 convert_element_type.20
  13.3 0.1 convert_element_type.22.m_ref
  13.4 0.0 copy-done.3
  13.4 0.1 reshape.133
  13.5 0.1 dynamic-slice_reduce_fusion
  13.6 0.1 eq.45
  13.7 0.0 copy-start.5
  13.7 0.0 copy-start.8
  13.7 23.1 %copy.25.ahead_ref.l_ref = bf16[40,641,640]{2,1,0:T(8,128)(2,1)} copy(bf16[40,641,640]{2,0,1:T(8,128)(2,1)} %param.13) | data formatting | bytes 65638400 | tf_op args[5]
  36.8 0.0 copy-done.5
  36.8 0.1 fusion.29
  36.9 0.0 copy-done.8
  36.9 0.0 copy-start.6
  36.9 0.0 copy-start.7
  36.9 3.8 %gather_fusion = s32[560]{0:T(1024)S(1)} fusion(s32[80]{0:T(128)S(1)} %get-tuple-element.29, s32[1024]{0:T(1024)S(1)} %pad_clamp_fusion), kind=kCustom, calls=%fused_computation | custom fusion | bytes 6720 | tf_op jit(solution)/shard_map/jit(_take)/gather | solution.py:607
  40.7 35.1 %tables.1 = (bf16[2,80,256,256]{3,2,1,0:T(8,128)(2,1)}, f32[2,80,32,128]{3,2,1,0:T(8,128)}, bf16[3,80,256,256]{3,2,1,0:T(8,128)(2,1)}, f32[3,80,32,128]{3,2,1,0:T(8,128)}) custom-call(f32[80]{0:T(128)S(1)} %add_convert_fusion.1.count_ref, f32[80]{0:T(128)S(1)} %broadcast_divide_fusion.inverse_ref, f32[80]{0:T(128)S(1)} %get-tuple-element.28.scale_ref, ...), custom_call_target="tpu_custom_call" | custom-call | flops 262144000 | bytes 52428800 | tf_op jit(solution)/shard_map/tables/pallas_call | solution.py:178
  75.9 0.0 copy-done.6
  75.9 0.0 copy-done.7
  75.9 0.3 select_reduce_fusion.slot_ref
  76.2 7.0 %all-to-all-done.a_ref = bf16[32,2,3,16,512]{4,3,2,1,0:T(8,128)(2,1)S(1)} async-done(((bf16[32,2,3,16,512]{4,3,2,1,0:T(8,128)(2,1)}), bf16[32,2,3,16,512]{4,3,2,1,0:T(8,128)(2,1)S(1)}, u32[]{:S(2)}, u32[]{:S(2)}) %all-to-all-start) | async-done | bytes 3145760 | tf_op jit(solution)/shard_map/all_to_all | solution.py:588
  83.1 0.0 copy-start
  83.2 1.7 copy-done
  84.9 17.3 %place_and_rows.1 = (bf16[640,768]{1,0:T(8,128)(2,1)}, bf16[8960,256]{1,0:T(8,128)(2,1)}) custom-call(s32[560]{0:T(1024)S(1)} %select_reduce_fusion.slot_ref, s32[560]{0:T(1024)S(1)} %get-tuple-element.30.room_ref, bf16[32,2,3,16,512]{4,3,2,1,0:T(8,128)(2,1)S(1)} %all-to-all-done.a_ref, bf16[40,641,640]{2,1,0:T(8,128)(2,1)} %copy.25.ahead_ref.l_ref, ...), custom_call_target="tpu_custom_call" | custom-call | flops 2348810240 | bytes 28180480 | tf_op jit(solution)/shard_map/place_and_rows/pallas_call | solution.py:340
  102.2 4.0 %all-to-all-start.2 = ((bf16[8,80,768]{2,1,0:T(8,128)(2,1)}), bf16[8,80,768]{2,1,0:T(8,128)(2,1)S(1)}, u32[]{:S(2)}, u32[]{:S(2)}) async-start(bf16[8,80,768]{2,1,0:T(8,128)(2,1)} %bitcast.23), calls=%async_computation.2 | async-start | bytes 1966080 | tf_op jit(solution)/shard_map/all_to_all | solution.py:630
  106.2 19.3 %rows_to_waves.1 = bf16[640,1152]{1,0:T(8,128)(2,1)} custom-call(bf16[8960,256]{1,0:T(8,128)(2,1)} %get-tuple-element.14.k_ref, bf16[3,80,256,256]{3,2,1,0:T(8,128)(2,1)} %get-tuple-element.15.t_ref, f32[3,80,32,128]{3,2,1,0:T(8,128)} %get-tuple-element.16.w_ref), custom_call_target="tpu_custom_call" | custom-call | flops 3523215360 | bytes 39976960 | tf_op jit(solution)/shard_map/rows_to_waves/pallas_call | solution.py:374
  125.5 0.0 all-to-all-done.2
  125.5 0.0 copy-start.2
  125.5 4.2 %all-to-all-start.1 = ((bf16[8,80,1152]{2,1,0:T(8,128)(2,1)}), bf16[8,80,1152]{2,1,0:T(8,128)(2,1)S(1)}, u32[]{:S(2)}, u32[]{:S(2)}) async-start(bf16[8,80,1152]{2,1,0:T(8,128)(2,1)} %bitcast.19), calls=%async_computation.1 | async-start | bytes 2949120 | tf_op jit(solution)/shard_map/all_to_all | solution.py:630
  129.7 0.6 dynamic_slice.10.own_ref
  130.4 1.1 fusion.p_ref
  131.5 0.0 copy-done.2
  131.5 14.7 %legendre.2 = (f32[40,12,641]{2,1,0:T(8,128)}, bf16[640,768]{1,0:T(8,128)(2,1)}) custom-call(s32[40]{0:T(128)} %dynamic_slice.10.own_ref, bf16[640,768]{1,0:T(8,128)(2,1)} %bitcast.20, bf16[640,640]{1,0:T(8,128)(2,1)} %fusion.p_ref, bf16[40,641,640]{2,1,0:T(8,128)(2,1)} %copy.25.ahead_ref.l_ref), custom_call_target="tpu_custom_call" | custom-call | flops 1260257280 | bytes 13127680 | tf_op jit(solution)/shard_map/legendre/pallas_call | solution.py:497
  146.2 3.5 %all-to-all-done.1 = bf16[8,80,1152]{2,1,0:T(8,128)(2,1)S(1)} async-done(((bf16[8,80,1152]{2,1,0:T(8,128)(2,1)}), bf16[8,80,1152]{2,1,0:T(8,128)(2,1)S(1)}, u32[]{:S(2)}, u32[]{:S(2)}) %all-to-all-start.1) | async-done | bytes 1474592 | tf_op jit(solution)/shard_map/all_to_all | solution.py:630
  149.7 0.0 copy-start.1
  149.7 3.6 %all-to-all-start.3 = ((bf16[8,80,768]{2,1,0:T(8,128)(2,1)}), bf16[8,80,768]{2,1,0:T(8,128)(2,1)S(1)}, u32[]{:S(2)}, u32[]{:S(2)}) async-start(bf16[8,80,768]{2,1,0:T(8,128)(2,1)} %bitcast.22), calls=%async_computation.3 | async-start | bytes 1966080 | tf_op jit(solution)/shard_map/all_to_all | solution.py:639
  153.3 0.0 copy-done.1
  153.3 20.2 %legendre.3 = (f32[40,12,641]{2,1,0:T(8,128)}, bf16[640,1152]{1,0:T(8,128)(2,1)}) custom-call(s32[40]{0:T(128)} %dynamic_slice.10.own_ref, bf16[640,1152]{1,0:T(8,128)(2,1)} %bitcast.18, bf16[640,640]{1,0:T(8,128)(2,1)} %fusion.p_ref, bf16[40,641,640]{2,1,0:T(8,128)(2,1)} %copy.25.ahead_ref.l_ref, ...), custom_call_target="tpu_custom_call", output_to_operand_aliasing={{0}: (4, {})} | custom-call | flops 1890385920 | bytes 19691520 | tf_op jit(solution)/shard_map/legendre/pallas_call | solution.py:497
  173.5 0.0 all-to-all-done.3.refs_0_
  173.5 4.1 %all-to-all-start.4 = ((bf16[8,80,1152]{2,1,0:T(8,128)(2,1)}), bf16[8,80,1152]{2,1,0:T(8,128)(2,1)S(1)}, u32[]{:S(2)}, u32[]{:S(2)}) async-start(bf16[8,80,1152]{2,1,0:T(8,128)(2,1)} %bitcast.21), calls=%async_computation.4 | async-start | bytes 2949120 | tf_op jit(solution)/shard_map/all_to_all | solution.py:639
  177.6 0.2 fusion.1.refs_2_
  177.8 2.4 %copy.28 = f32[40,12,641]{2,0,1:T(8,128)S(1)} copy(f32[40,12,641]{2,1,0:T(8,128)} %get-tuple-element.19) | data formatting | bytes 2461440 | tf_op jit(solution)/shard_map/legendre/pallas_call | solution.py:497
  180.2 1.9 copy.29
  182.1 15.5 %all-to-all-done.4.refs_1_ = bf16[8,80,1152]{2,1,0:T(8,128)(2,1)S(1)} async-done(((bf16[8,80,1152]{2,1,0:T(8,128)(2,1)}), bf16[8,80,1152]{2,1,0:T(8,128)(2,1)S(1)}, u32[]{:S(2)}, u32[]{:S(2)}) %all-to-all-start.4) | async-done | bytes 1474592 | tf_op jit(solution)/shard_map/all_to_all | solution.py:639
  197.6 5.7 %unpack.1 = bf16[24,80,640]{2,1,0:T(8,128)(2,1)S(1)} custom-call(bf16[8,80,768]{2,1,0:T(8,128)(2,1)S(1)} %all-to-all-done.3.refs_0_, bf16[8,80,1152]{2,1,0:T(8,128)(2,1)S(1)} %all-to-all-done.4.refs_1_, bf16[640,640]{1,0:T(8,128)(2,1)S(1)} %fusion.1.refs_2_), custom_call_target="tpu_custom_call" | custom-call | flops 1572864000 | bytes 4915200 | tf_op jit(solution)/shard_map/unpack/pallas_call | solution.py:554
  203.3 3.3 %copy.30 = bf16[80,2,2,3,2,640]{5,4,3,2,1,0:T(2,128)(2,1)} copy(bf16[80,2,2,3,2,640]{5,0,4,3,2,1:T(8,128)(2,1)S(1)} %bitcast.14) | data formatting | bytes 4915200
  (10 shorter events, 0.1 us)
Async XLA Ops:
  5.7 7.3 %copy-start.4 = (s32[320]{0:T(512)S(1)}, s32[320]{0:T(512)}, u32[]{:S(2)}) copy-start(s32[320]{0:T(512)} %param.12) | copy-start | bytes 3844
  5.7 7.7 %copy-start.3 = (s32[4096]{0:T(1024)S(1)}, s32[4096]{0:T(1024)}, u32[]{:S(2)}) copy-start(s32[4096]{0:T(1024)} %param.10) | copy-start | bytes 49156
  5.7 77.5 %all-to-all-start = ((bf16[32,2,3,16,512]{4,3,2,1,0:T(8,128)(2,1)}), bf16[32,2,3,16,512]{4,3,2,1,0:T(8,128)(2,1)S(1)}, u32[]{:S(2)}, u32[]{:S(2)}) async-start(bf16[32,2,3,16,512]{4,3,2,1,0:T(8,128)(2,1)} %bitcast.15), calls=%async_computation | async-start | bytes 6291456 | tf_op jit(solution)/shard_map/all_to_all | solution.py:588
  13.7 23.1 %copy-start.5 = (s32[640]{0:T(1024)S(1)}, s32[640]{0:T(1024)}, u32[]{:S(2)}) copy-start(s32[640]{0:T(1024)} %param.11) | copy-start | bytes 7684
  13.7 23.2 %copy-start.8 = (s32[560]{0:T(1024)S(1)}, s32[560]{0:T(1024)}, u32[]{:S(2)}) copy-start(s32[560]{0:T(1024)} %constant.137) | copy-start | bytes 6724
  36.9 39.0 %copy-start.6 = (s32[560]{0:T(1024)S(1)}, s32[560]{0:T(1024)}, u32[]{:S(2)}) copy-start(s32[560]{0:T(1024)} %constant.126.clone) | copy-start | bytes 6724
  36.9 39.0 %copy-start.7 = (s32[560]{0:T(1024)S(1)}, s32[560]{0:T(1024)}, u32[]{:S(2)}) copy-start(s32[560]{0:T(1024)} %constant.136) | copy-start | bytes 6724
  83.1 1.7 copy-start
  102.2 23.3 %all-to-all-start.2 = ((bf16[8,80,768]{2,1,0:T(8,128)(2,1)}), bf16[8,80,768]{2,1,0:T(8,128)(2,1)S(1)}, u32[]{:S(2)}, u32[]{:S(2)}) async-start(bf16[8,80,768]{2,1,0:T(8,128)(2,1)} %bitcast.23), calls=%async_computation.2 | async-start | bytes 1966080 | tf_op jit(solution)/shard_map/all_to_all | solution.py:630
  125.5 6.0 %copy-start.2 = (bf16[8,80,768]{2,1,0:T(8,128)(2,1)}, bf16[8,80,768]{2,1,0:T(8,128)(2,1)S(1)}, u32[]{:S(2)}) copy-start(bf16[8,80,768]{2,1,0:T(8,128)(2,1)S(1)} %all-to-all-done.2) | copy-start | bytes 2949124
  125.5 24.2 %all-to-all-start.1 = ((bf16[8,80,1152]{2,1,0:T(8,128)(2,1)}), bf16[8,80,1152]{2,1,0:T(8,128)(2,1)S(1)}, u32[]{:S(2)}, u32[]{:S(2)}) async-start(bf16[8,80,1152]{2,1,0:T(8,128)(2,1)} %bitcast.19), calls=%async_computation.1 | async-start | bytes 2949120 | tf_op jit(solution)/shard_map/all_to_all | solution.py:630
  149.7 3.6 %copy-start.1 = (bf16[8,80,1152]{2,1,0:T(8,128)(2,1)}, bf16[8,80,1152]{2,1,0:T(8,128)(2,1)S(1)}, u32[]{:S(2)}) copy-start(bf16[8,80,1152]{2,1,0:T(8,128)(2,1)S(1)} %all-to-all-done.1) | copy-start | bytes 4423684
  149.7 23.8 %all-to-all-start.3 = ((bf16[8,80,768]{2,1,0:T(8,128)(2,1)}), bf16[8,80,768]{2,1,0:T(8,128)(2,1)S(1)}, u32[]{:S(2)}, u32[]{:S(2)}) async-start(bf16[8,80,768]{2,1,0:T(8,128)(2,1)} %bitcast.22), calls=%async_computation.3 | async-start | bytes 1966080 | tf_op jit(solution)/shard_map/all_to_all | solution.py:639
  173.5 24.1 %all-to-all-start.4 = ((bf16[8,80,1152]{2,1,0:T(8,128)(2,1)}), bf16[8,80,1152]{2,1,0:T(8,128)(2,1)S(1)}, u32[]{:S(2)}, u32[]{:S(2)}) async-start(bf16[8,80,1152]{2,1,0:T(8,128)(2,1)} %bitcast.21), calls=%async_computation.4 | async-start | bytes 2949120 | tf_op jit(solution)/shard_map/all_to_all | solution.py:639

commit v4 on v3

--- a/solution.py
+++ b/solution.py
@@ -479,7 +479,7 @@
     cgs = -(-4 * lf // waves)
     rows = cgs * LANE
     per_group = LANE // waves // 2
-    many = 4
+    many = min(8, per_group)
     stages = per_group // many
     g0, ng = chunk
     block = lambda g, k, *_: ((g0 + g) * stages + k, 0, 0)

time: 207 us -> 207 us (level)
  no operation moved by 1% of the time
where the time goes in v4:
time: 207 us; the launch traced here: 206 us
  Pallas kernels  116 us (56%)
  local copies, waits for them, and re-layouts  37.5 us (18%)
  waiting for transfers between devices  26.1 us (13%)
  starting transfers between devices  23.2 us (11%)
    pallas_call x1, Pallas kernels, phase_tables(): pl.pallas_call(functools.partial(table_kernel, chunks), grid_spec=pltpu.P...  35.1 us
    pallas_call x2, Pallas kernels, legendre_both(): pl.pallas_call(functools.partial(legendre_kernel, g0, per_group, waves, l...  34.1 us
    unnamed x21, local copies, waits for them, and re-layouts  30.1 us
    pallas_call x1, Pallas kernels, rows_to_waves(): pl.pallas_call(functools.partial(rows_kernel, blocks, lf, waves, pairs),...  19.3 us
    pallas_call x1, Pallas kernels, first_rows(): pl.pallas_call(functools.partial(first_kernel, blocks, lf, waves, pairs),...  17.3 us
    all_to_all x2, waiting for transfers between devices, body(): returned.append(lax.all_to_all(back, 'wave', 0, 0, tiled=True))  15.5 us
    all_to_all x2, starting transfers between devices, body(): received.append(lax.all_to_all(sent, 'wave', 0, 0, tiled=True))  8.25 us
    all_to_all x2, starting transfers between devices, body(): returned.append(lax.all_to_all(back, 'wave', 0, 0, tiled=True))  7.67 us
  transfers between devices with their start and end apart: 5, of which 3 were waited for; matrix products, arithmetic and copies ran while one was open for 17% of the time, Pallas kernels for 43%

profile of v4, /device:TPU:0, one launch (start us, length us, event | category | flops | bytes accessed | tf_op | source)
XLA Modules:
  0.0 205.9 jit_solution(16682545941676985977)
XLA Ops:
  0.6 5.0 %diffuse.1 = bf16[8,4,2,3,16,512]{5,4,3,2,1,0:T(8,128)(2,1)} custom-call(f32[8,3,8,16,512]{4,3,2,1,0:T(8,128)} %bitcast.16, bf16[7,8,16,512]{3,2,1,0:T(8,128)(2,1)} %bitcast.24), custom_call_target="tpu_custom_call" | custom-call | flops 62914560 | bytes 10354688 | tf_op jit(solution)/shard_map/diffuse/pallas_call | solution.py:101
  5.7 0.0 copy-start.4
  5.7 0.0 copy-start.3
  5.7 7.3 %all-to-all-start = ((bf16[32,2,3,16,512]{4,3,2,1,0:T(8,128)(2,1)}), bf16[32,2,3,16,512]{4,3,2,1,0:T(8,128)(2,1)S(1)}, u32[]{:S(2)}, u32[]{:S(2)}) async-start(bf16[32,2,3,16,512]{4,3,2,1,0:T(8,128)(2,1)} %bitcast.15), calls=%async_computation | async-start | bytes 6291456 | tf_op jit(solution)/shard_map/all_to_all | solution.py:588
  13.0 0.0 copy-done.4
  13.1 0.1 copy.23
  13.2 0.1 convert_element_type.20
  13.3 0.1 convert_element_type.22.m_ref
  13.4 0.0 copy-done.3
  13.4 0.1 reshape.133
  13.5 0.1 dynamic-slice_reduce_fusion
  13.6 0.1 eq.45
  13.7 0.0 copy-start.5
  13.7 0.0 copy-start.8
  13.7 23.1 %copy.25.ahead_ref.l_ref = bf16[40,641,640]{2,1,0:T(8,128)(2,1)} copy(bf16[40,641,640]{2,0,1:T(8,128)(2,1)} %param.13) | data formatting | bytes 65638400 | tf_op args[5]
  36.8 0.0 copy-done.5
  36.8 0.1 fusion.29
  36.9 0.0 copy-done.8
  36.9 0.0 copy-start.6
  36.9 0.0 copy-start.7
  36.9 3.8 %gather_fusion = s32[560]{0:T(1024)S(1)} fusion(s32[80]{0:T(128)S(1)} %get-tuple-element.29, s32[1024]{0:T(1024)S(1)} %pad_clamp_fusion), kind=kCustom, calls=%fused_computation | custom fusion | bytes 6720 | tf_op jit(solution)/shard_map/jit(_take)/gather | solution.py:607
  40.7 35.1 %tables.1 = (bf16[2,80,256,256]{3,2,1,0:T(8,128)(2,1)}, f32[2,80,32,128]{3,2,1,0:T(8,128)}, bf16[3,80,256,256]{3,2,1,0:T(8,128)(2,1)}, f32[3,80,32,128]{3,2,1,0:T(8,128)}) custom-call(f32[80]{0:T(128)S(1)} %add_convert_fusion.1.count_ref, f32[80]{0:T(128)S(1)} %broadcast_divide_fusion.inverse_ref, f32[80]{0:T(128)S(1)} %get-tuple-element.28.scale_ref, ...), custom_call_target="tpu_custom_call" | custom-call | flops 262144000 | bytes 52428800 | tf_op jit(solution)/shard_map/tables/pallas_call | solution.py:178
  75.9 0.0 copy-done.6
  75.9 0.0 copy-done.7
  75.9 0.3 select_reduce_fusion.slot_ref
  76.2 7.0 %all-to-all-done.a_ref = bf16[32,2,3,16,512]{4,3,2,1,0:T(8,128)(2,1)S(1)} async-done(((bf16[32,2,3,16,512]{4,3,2,1,0:T(8,128)(2,1)}), bf16[32,2,3,16,512]{4,3,2,1,0:T(8,128)(2,1)S(1)}, u32[]{:S(2)}, u32[]{:S(2)}) %all-to-all-start) | async-done | bytes 3145760 | tf_op jit(solution)/shard_map/all_to_all | solution.py:588
  83.1 0.0 copy-start
  83.2 1.7 copy-done
  84.9 17.3 %place_and_rows.1 = (bf16[640,768]{1,0:T(8,128)(2,1)}, bf16[8960,256]{1,0:T(8,128)(2,1)}) custom-call(s32[560]{0:T(1024)S(1)} %select_reduce_fusion.slot_ref, s32[560]{0:T(1024)S(1)} %get-tuple-element.30.room_ref, bf16[32,2,3,16,512]{4,3,2,1,0:T(8,128)(2,1)S(1)} %all-to-all-done.a_ref, bf16[40,641,640]{2,1,0:T(8,128)(2,1)} %copy.25.ahead_ref.l_ref, ...), custom_call_target="tpu_custom_call" | custom-call | flops 2348810240 | bytes 28180480 | tf_op jit(solution)/shard_map/place_and_rows/pallas_call | solution.py:340
  102.2 4.0 %all-to-all-start.2 = ((bf16[8,80,768]{2,1,0:T(8,128)(2,1)}), bf16[8,80,768]{2,1,0:T(8,128)(2,1)S(1)}, u32[]{:S(2)}, u32[]{:S(2)}) async-start(bf16[8,80,768]{2,1,0:T(8,128)(2,1)} %bitcast.23), calls=%async_computation.2 | async-start | bytes 1966080 | tf_op jit(solution)/shard_map/all_to_all | solution.py:630
  106.2 19.3 %rows_to_waves.1 = bf16[640,1152]{1,0:T(8,128)(2,1)} custom-call(bf16[8960,256]{1,0:T(8,128)(2,1)} %get-tuple-element.14.k_ref, bf16[3,80,256,256]{3,2,1,0:T(8,128)(2,1)} %get-tuple-element.15.t_ref, f32[3,80,32,128]{3,2,1,0:T(8,128)} %get-tuple-element.16.w_ref), custom_call_target="tpu_custom_call" | custom-call | flops 3523215360 | bytes 39976960 | tf_op jit(solution)/shard_map/rows_to_waves/pallas_call | solution.py:374
  125.5 0.0 all-to-all-done.2
  125.5 0.0 copy-start.2
  125.5 4.2 %all-to-all-start.1 = ((bf16[8,80,1152]{2,1,0:T(8,128)(2,1)}), bf16[8,80,1152]{2,1,0:T(8,128)(2,1)S(1)}, u32[]{:S(2)}, u32[]{:S(2)}) async-start(bf16[8,80,1152]{2,1,0:T(8,128)(2,1)} %bitcast.19), calls=%async_computation.1 | async-start | bytes 2949120 | tf_op jit(solution)/shard_map/all_to_all | solution.py:630
  129.7 0.6 dynamic_slice.10.own_ref
  130.4 1.1 fusion.p_ref
  131.5 0.0 copy-done.2
  131.5 14.5 %legendre.2 = (f32[40,12,641]{2,1,0:T(8,128)}, bf16[640,768]{1,0:T(8,128)(2,1)}) custom-call(s32[40]{0:T(128)} %dynamic_slice.10.own_ref, bf16[640,768]{1,0:T(8,128)(2,1)} %bitcast.20, bf16[640,640]{1,0:T(8,128)(2,1)} %fusion.p_ref, bf16[40,641,640]{2,1,0:T(8,128)(2,1)} %copy.25.ahead_ref.l_ref), custom_call_target="tpu_custom_call" | custom-call | flops 1260257280 | bytes 13127680 | tf_op jit(solution)/shard_map/legendre/pallas_call | solution.py:497
  146.1 3.7 %all-to-all-done.1 = bf16[8,80,1152]{2,1,0:T(8,128)(2,1)S(1)} async-done(((bf16[8,80,1152]{2,1,0:T(8,128)(2,1)}), bf16[8,80,1152]{2,1,0:T(8,128)(2,1)S(1)}, u32[]{:S(2)}, u32[]{:S(2)}) %all-to-all-start.1) | async-done | bytes 1474592 | tf_op jit(solution)/shard_map/all_to_all | solution.py:630
  149.7 0.0 copy-start.1
  149.7 3.6 %all-to-all-start.3 = ((bf16[8,80,768]{2,1,0:T(8,128)(2,1)}), bf16[8,80,768]{2,1,0:T(8,128)(2,1)S(1)}, u32[]{:S(2)}, u32[]{:S(2)}) async-start(bf16[8,80,768]{2,1,0:T(8,128)(2,1)} %bitcast.22), calls=%async_computation.3 | async-start | bytes 1966080 | tf_op jit(solution)/shard_map/all_to_all | solution.py:639
  153.3 0.0 copy-done.1
  153.3 19.5 %legendre.3 = (f32[40,12,641]{2,1,0:T(8,128)}, bf16[640,1152]{1,0:T(8,128)(2,1)}) custom-call(s32[40]{0:T(128)} %dynamic_slice.10.own_ref, bf16[640,1152]{1,0:T(8,128)(2,1)} %bitcast.18, bf16[640,640]{1,0:T(8,128)(2,1)} %fusion.p_ref, bf16[40,641,640]{2,1,0:T(8,128)(2,1)} %copy.25.ahead_ref.l_ref, ...), custom_call_target="tpu_custom_call", output_to_operand_aliasing={{0}: (4, {})} | custom-call | flops 1890385920 | bytes 19691520 | tf_op jit(solution)/shard_map/legendre/pallas_call | solution.py:497
  172.8 0.0 all-to-all-done.3.refs_0_
  172.8 4.1 %all-to-all-start.4 = ((bf16[8,80,1152]{2,1,0:T(8,128)(2,1)}), bf16[8,80,1152]{2,1,0:T(8,128)(2,1)S(1)}, u32[]{:S(2)}, u32[]{:S(2)}) async-start(bf16[8,80,1152]{2,1,0:T(8,128)(2,1)} %bitcast.21), calls=%async_computation.4 | async-start | bytes 2949120 | tf_op jit(solution)/shard_map/all_to_all | solution.py:639
  176.9 0.2 fusion.1.refs_2_
  177.2 2.4 %copy.28 = f32[40,12,641]{2,0,1:T(8,128)S(1)} copy(f32[40,12,641]{2,1,0:T(8,128)} %get-tuple-element.19) | data formatting | bytes 2461440 | tf_op jit(solution)/shard_map/legendre/pallas_call | solution.py:497
  179.6 1.9 copy.29
  181.4 15.5 %all-to-all-done.4.refs_1_ = bf16[8,80,1152]{2,1,0:T(8,128)(2,1)S(1)} async-done(((bf16[8,80,1152]{2,1,0:T(8,128)(2,1)}), bf16[8,80,1152]{2,1,0:T(8,128)(2,1)S(1)}, u32[]{:S(2)}, u32[]{:S(2)}) %all-to-all-start.4) | async-done | bytes 1474592 | tf_op jit(solution)/shard_map/all_to_all | solution.py:639
  196.9 5.7 %unpack.1 = bf16[24,80,640]{2,1,0:T(8,128)(2,1)S(1)} custom-call(bf16[8,80,768]{2,1,0:T(8,128)(2,1)S(1)} %all-to-all-done.3.refs_0_, bf16[8,80,1152]{2,1,0:T(8,128)(2,1)S(1)} %all-to-all-done.4.refs_1_, bf16[640,640]{1,0:T(8,128)(2,1)S(1)} %fusion.1.refs_2_), custom_call_target="tpu_custom_call" | custom-call | flops 1572864000 | bytes 4915200 | tf_op jit(solution)/shard_map/unpack/pallas_call | solution.py:554
  202.6 3.3 %copy.30 = bf16[80,2,2,3,2,640]{5,4,3,2,1,0:T(2,128)(2,1)} copy(bf16[80,2,2,3,2,640]{5,0,4,3,2,1:T(8,128)(2,1)S(1)} %bitcast.14) | data formatting | bytes 4915200
  (10 shorter events, 0.1 us)
Async XLA Ops:
  5.7 7.3 %copy-start.4 = (s32[320]{0:T(512)S(1)}, s32[320]{0:T(512)}, u32[]{:S(2)}) copy-start(s32[320]{0:T(512)} %param.12) | copy-start | bytes 3844
  5.7 7.7 %copy-start.3 = (s32[4096]{0:T(1024)S(1)}, s32[4096]{0:T(1024)}, u32[]{:S(2)}) copy-start(s32[4096]{0:T(1024)} %param.10) | copy-start | bytes 49156
  5.7 77.5 %all-to-all-start = ((bf16[32,2,3,16,512]{4,3,2,1,0:T(8,128)(2,1)}), bf16[32,2,3,16,512]{4,3,2,1,0:T(8,128)(2,1)S(1)}, u32[]{:S(2)}, u32[]{:S(2)}) async-start(bf16[32,2,3,16,512]{4,3,2,1,0:T(8,128)(2,1)} %bitcast.15), calls=%async_computation | async-start | bytes 6291456 | tf_op jit(solution)/shard_map/all_to_all | solution.py:588
  13.7 23.1 %copy-start.5 = (s32[640]{0:T(1024)S(1)}, s32[640]{0:T(1024)}, u32[]{:S(2)}) copy-start(s32[640]{0:T(1024)} %param.11) | copy-start | bytes 7684
  13.7 23.2 %copy-start.8 = (s32[560]{0:T(1024)S(1)}, s32[560]{0:T(1024)}, u32[]{:S(2)}) copy-start(s32[560]{0:T(1024)} %constant.137) | copy-start | bytes 6724
  36.9 39.0 %copy-start.6 = (s32[560]{0:T(1024)S(1)}, s32[560]{0:T(1024)}, u32[]{:S(2)}) copy-start(s32[560]{0:T(1024)} %constant.126.clone) | copy-start | bytes 6724
  36.9 39.0 %copy-start.7 = (s32[560]{0:T(1024)S(1)}, s32[560]{0:T(1024)}, u32[]{:S(2)}) copy-start(s32[560]{0:T(1024)} %constant.136) | copy-start | bytes 6724
  83.1 1.7 copy-start
  102.2 23.3 %all-to-all-start.2 = ((bf16[8,80,768]{2,1,0:T(8,128)(2,1)}), bf16[8,80,768]{2,1,0:T(8,128)(2,1)S(1)}, u32[]{:S(2)}, u32[]{:S(2)}) async-start(bf16[8,80,768]{2,1,0:T(8,128)(2,1)} %bitcast.23), calls=%async_computation.2 | async-start | bytes 1966080 | tf_op jit(solution)/shard_map/all_to_all | solution.py:630
  125.5 6.0 %copy-start.2 = (bf16[8,80,768]{2,1,0:T(8,128)(2,1)}, bf16[8,80,768]{2,1,0:T(8,128)(2,1)S(1)}, u32[]{:S(2)}) copy-start(bf16[8,80,768]{2,1,0:T(8,128)(2,1)S(1)} %all-to-all-done.2) | copy-start | bytes 2949124
  125.5 24.2 %all-to-all-start.1 = ((bf16[8,80,1152]{2,1,0:T(8,128)(2,1)}), bf16[8,80,1152]{2,1,0:T(8,128)(2,1)S(1)}, u32[]{:S(2)}, u32[]{:S(2)}) async-start(bf16[8,80,1152]{2,1,0:T(8,128)(2,1)} %bitcast.19), calls=%async_computation.1 | async-start | bytes 2949120 | tf_op jit(solution)/shard_map/all_to_all | solution.py:630
  149.7 3.6 %copy-start.1 = (bf16[8,80,1152]{2,1,0:T(8,128)(2,1)}, bf16[8,80,1152]{2,1,0:T(8,128)(2,1)S(1)}, u32[]{:S(2)}) copy-start(bf16[8,80,1152]{2,1,0:T(8,128)(2,1)S(1)} %all-to-all-done.1) | copy-start | bytes 4423684
  149.7 23.1 %all-to-all-start.3 = ((bf16[8,80,768]{2,1,0:T(8,128)(2,1)}), bf16[8,80,768]{2,1,0:T(8,128)(2,1)S(1)}, u32[]{:S(2)}, u32[]{:S(2)}) async-start(bf16[8,80,768]{2,1,0:T(8,128)(2,1)} %bitcast.22), calls=%async_computation.3 | async-start | bytes 1966080 | tf_op jit(solution)/shard_map/all_to_all | solution.py:639
  172.8 24.1 %all-to-all-start.4 = ((bf16[8,80,1152]{2,1,0:T(8,128)(2,1)}), bf16[8,80,1152]{2,1,0:T(8,128)(2,1)S(1)}, u32[]{:S(2)}, u32[]{:S(2)}) async-start(bf16[8,80,1152]{2,1,0:T(8,128)(2,1)} %bitcast.21), calls=%async_computation.4 | async-start | bytes 2949120 | tf_op jit(solution)/shard_map/all_to_all | solution.py:639
